TPU v7x, 32 devices: a whole 2x2x4 slice. The times are simulated.
32 devices in a mesh: ctx: 16 (over z, y, x), head: 2 (over core).
Axes of the slice: x: 2, y: 2, z: 4, core: 2. Of those that a mesh axis runs over, the one named last changes fastest.
Arguments:
- hidden_in: bfloat16 [2048, 2304], P('ctx'), may hold values from -6 to 6
- out_cotangent: bfloat16 [2048, 2304], P('ctx'), may hold values from -6 to 6
- block_table: int32 [16, 2], replicated, may hold values from 0 to 31, as said below
- attend_weight: float32 [2304, 4, 4, 256], P('ctx', 'head'), may hold values from -0.1875 to 0.1875
- attend_moment: float32 [2304, 4, 4, 256], P('ctx', 'head'), may hold values from -14.934095 to 14.934095
- attend_square: float32 [2304, 4, 4, 256], P('ctx', 'head'), may hold values from 26.624 to 108.544
- output_weight: float32 [8, 256, 2304], P('head', None, 'ctx'), may hold values from -0.25 to 0.25
- output_moment: float32 [8, 256, 2304], P('head', None, 'ctx'), may hold values from -14.934095 to 14.934095
- output_square: float32 [8, 256, 2304], P('head', None, 'ctx'), may hold values from 26.624 to 108.544
- expand_weight: float32 [2304, 2, 9216], P('ctx', None, 'head'), may hold values from -0.125 to 0.125
- expand_moment: float32 [2304, 2, 9216], P('ctx', None, 'head'), may hold values from -14.934095 to 14.934095
- expand_square: float32 [2304, 2, 9216], P('ctx', None, 'head'), may hold values from 26.624 to 108.544
- shrink_weight: float32 [9216, 2304], P('head', 'ctx'), may hold values from -0.0625 to 0.0625
- shrink_moment: float32 [9216, 2304], P('head', 'ctx'), may hold values from -14.934095 to 14.934095
- shrink_square: float32 [9216, 2304], P('head', 'ctx'), may hold values from 26.624 to 108.544
- gains_weight: float32 [4, 2304], P(None, 'ctx'), may hold values from -0.8 to 0.8
- gains_moment: float32 [4, 2304], P(None, 'ctx'), may hold values from -29.86819 to 29.86819
- gains_square: float32 [4, 2304], P(None, 'ctx'), may hold values from 108.544 to 430.08
Outputs:
- hidden_out: bfloat16 [2048, 2304], P('ctx')
- hidden_grad: float32 [2048, 2304], P('ctx')
- attend_grad: float32 [2304, 4, 4, 256], P('ctx', 'head')
- attend_after: float32 [2304, 4, 4, 256], P('ctx', 'head')
- attend_mean: float32 [2304, 4, 4, 256], P('ctx', 'head')
- attend_power: float32 [2304, 4, 4, 256], P('ctx', 'head')
- output_grad: float32 [8, 256, 2304], P('head', None, 'ctx')
- output_after: float32 [8, 256, 2304], P('head', None, 'ctx')
- output_mean: float32 [8, 256, 2304], P('head', None, 'ctx')
- output_power: float32 [8, 256, 2304], P('head', None, 'ctx')
- expand_grad: float32 [2304, 2, 9216], P('ctx', None, 'head')
- expand_after: float32 [2304, 2, 9216], P('ctx', None, 'head')
- expand_mean: float32 [2304, 2, 9216], P('ctx', None, 'head')
- expand_power: float32 [2304, 2, 9216], P('ctx', None, 'head')
- shrink_grad: float32 [9216, 2304], P('head', 'ctx')
- shrink_after: float32 [9216, 2304], P('head', 'ctx')
- shrink_mean: float32 [9216, 2304], P('head', 'ctx')
- shrink_power: float32 [9216, 2304], P('head', 'ctx')
- gains_grad: float32 [4, 2304], P(None, 'ctx')
- gains_after: float32 [4, 2304], P(None, 'ctx')
- gains_mean: float32 [4, 2304], P(None, 'ctx')
- gains_power: float32 [4, 2304], P(None, 'ctx')
Inputs may be any that keep to these rules, and one draw needn't show every extreme that they name: `block_table`: row i lists the two blocks of 64 tokens held by index i of ctx, in the order in which they are laid end to end; the two numbers of a row add up to 31 and every block appears once.
All inputs are finite; a program needn't handle non-finite values.
Results may differ from a plain program's by a relative error of at most 0.02.
The roundings to bfloat16 on the way count: a program that leaves them out, or rounds other values in their place, can miss the bound.
Values may be sent and summed in bfloat16 or wider, within the bound.
No kernel may reach another device: no remote copies, remote signals or barrier semaphores. Data moves between devices by JAX's collectives and lax.ppermute only.
A program may use at most 256 MiB of HBM per device.

v0:
```python
import jax
import jax.numpy as jnp
from jax import lax
from jax.sharding import PartitionSpec as P

STEP = 10


NORM_EPS = 1e-06
SOFT_CAP = 50.0
ROPE_BASE = 10000.0
RATE_MATRIX = 0.02
RATE_GAIN = 0.1
BETA_ONE = 0.9
BETA_TWO = 0.95
ADAM_EPS = 1e-08
DECAY = 0.1
CONTRACT_ROWS = (((0,), (0,)), ((), ()))
CONTRACT_LAST = (((1,), (1,)), ((), ()))


def rope_tables(positions, head_width):
    exponent = jnp.arange(head_width // 2, dtype=jnp.float32) * (2.0 / head_width)
    frequency = ROPE_BASE ** (-exponent)
    angle = positions.astype(jnp.float32)[:, None] * frequency[None, :]
    return (jnp.cos(angle), jnp.sin(angle))


def rotate(values, cosine, sine_table):
    middle = values.shape[-1] // 2
    front_half = values[..., :middle]
    back_half = values[..., middle:]
    return jnp.concatenate(
        [
            front_half * cosine - back_half * sine_table,
            back_half * cosine + front_half * sine_table,
        ],
        axis=-1,
    )


def norm_apply(values, norm_gain):
    return (
        values
        * lax.rsqrt(jnp.mean(values * values, axis=-1, keepdims=True) + NORM_EPS)
        * (1.0 + norm_gain)
    )


def norm_back(values, norm_gain, grad_out):
    factor = lax.rsqrt(jnp.mean(values * values, axis=-1, keepdims=True) + NORM_EPS)
    weighted = grad_out * (1.0 + norm_gain)
    grad_in = factor * weighted - values * factor * factor * factor * jnp.mean(
        values * weighted, axis=-1, keepdims=True
    )
    grad_gain = jnp.sum(grad_out * values * factor, axis=0)
    return (grad_in, grad_gain)


def gate_product(gate_act, up_act):
    return jax.nn.gelu(gate_act, approximate=True) * up_act


def adam_step(weight, moment, square, grad, rate, decay):
    moment_new = BETA_ONE * moment + (1.0 - BETA_ONE) * grad
    square_new = BETA_TWO * square + (1.0 - BETA_TWO) * grad * grad
    mean_hat = moment_new / (1.0 - BETA_ONE**STEP)
    power_hat = square_new / (1.0 - BETA_TWO**STEP)
    updated = weight - rate * (mean_hat / (jnp.sqrt(power_hat) + ADAM_EPS) + decay * weight)
    return (updated, moment_new, square_new)


def score_block(queries, keys_part, query_spot, key_spot, score_scale):
    raw_score = jnp.einsum("qgjd,kgd->gjqk", queries, keys_part, preferred_element_type=jnp.float32)
    bent_score = jnp.tanh(raw_score * score_scale / SOFT_CAP)
    allowed = key_spot[None, :] <= query_spot[:, None]
    exp_score = jnp.where(allowed[None, None], jnp.exp(SOFT_CAP * bent_score), 0.0)
    return (exp_score, bent_score)


def pack_weights(attend_weight, output_weight, expand_weight, shrink_weight):
    local_width = attend_weight.shape[0]
    return (
        attend_weight.astype(jnp.bfloat16).reshape(local_width, -1),
        output_weight.astype(jnp.bfloat16).reshape(-1, local_width).T,
        expand_weight.astype(jnp.bfloat16).reshape(local_width, -1),
        shrink_weight.astype(jnp.bfloat16).T,
    )


def column_sums(factor_pairs, local_width, block_cols, sender):
    results = []
    for left_side, right_side in factor_pairs:
        col_count = right_side.shape[1]

        def column_turn(block_index, running):
            first_col = block_index * block_cols
            column_part = lax.dynamic_slice_in_dim(right_side, first_col, block_cols, 1)
            partial_value = lax.dot_general(
                left_side, column_part, CONTRACT_ROWS, preferred_element_type=jnp.float32
            )
            return lax.dynamic_update_slice_in_dim(running, sender(partial_value), first_col, 1)

        start_sums = jnp.zeros((local_width, col_count), jnp.float32)
        results.append(lax.fori_loop(0, col_count // block_cols, column_turn, start_sums))
    return jnp.concatenate(results, axis=1)


def body(
    hidden_in,
    out_cotangent,
    block_table,
    attend_weight,
    attend_moment,
    attend_square,
    output_weight,
    output_moment,
    output_square,
    expand_weight,
    expand_moment,
    expand_square,
    shrink_weight,
    shrink_moment,
    shrink_square,
    gains_weight,
    gains_moment,
    gains_square,
):
    shard_count = lax.axis_size("ctx")
    ctx_rank = lax.axis_index("ctx")
    tok_rows = hidden_in.shape[0]
    local_width = attend_weight.shape[0]
    group_count = attend_weight.shape[1]
    slot_count = attend_weight.shape[2]
    pair_count = slot_count - 2
    head_width = attend_weight.shape[3]
    hidden_width = expand_weight.shape[2]
    length = tok_rows * shard_count
    half_rows = tok_rows // 2
    score_scale = head_width ** (-0.5)
    block_cols = 2 * head_width

    def send_all(partial_value):
        return (
            lax.all_to_all(
                partial_value.reshape(shard_count, local_width, -1).astype(jnp.bfloat16),
                "ctx",
                split_axis=0,
                concat_axis=0,
                tiled=True,
            )
            .astype(jnp.float32)
            .sum(axis=0)
        )

    offsets = jnp.arange(half_rows, dtype=jnp.int32)
    all_spots = (block_table[:, :, None] * half_rows + offsets[None, None, :]).reshape(length)
    own_spots = lax.dynamic_slice_in_dim(all_spots, ctx_rank * tok_rows, tok_rows)
    packed = pack_weights(attend_weight, output_weight, expand_weight, shrink_weight)
    attend_full, output_full, expand_full, shrink_full, gains_full = (
        lax.all_gather(packed[0], "ctx", axis=0, tiled=True),
        lax.all_gather(packed[1], "ctx", axis=0, tiled=True),
        lax.all_gather(packed[2], "ctx", axis=0, tiled=True),
        lax.all_gather(packed[3], "ctx", axis=0, tiled=True),
        lax.all_gather(gains_weight.astype(jnp.bfloat16), "ctx", axis=1, tiled=True),
    )
    gains_all = gains_full.astype(jnp.float32)
    hidden = hidden_in.astype(jnp.float32)
    normed_b = norm_apply(hidden, gains_all[0]).astype(jnp.bfloat16)
    projected = jnp.dot(normed_b, attend_full, preferred_element_type=jnp.float32).reshape(
        tok_rows, group_count, slot_count, head_width
    )
    cosine, sine_table = rope_tables(own_spots, head_width)
    queries_b = rotate(
        projected[:, :, :pair_count], cosine[:, None, None], sine_table[:, None, None]
    ).astype(jnp.bfloat16)
    keys_b = rotate(projected[:, :, pair_count], cosine[:, None], sine_table[:, None]).astype(
        jnp.bfloat16
    )
    values_b = projected[:, :, pair_count + 1].astype(jnp.bfloat16)
    own_pairs = jnp.stack([keys_b, values_b], axis=1).reshape(tok_rows, -1)
    gathered = lax.all_gather(own_pairs, "ctx", axis=0, tiled=True).reshape(
        length, 2, group_count, head_width
    )
    key_block = min(2048, length)
    block_count = length // key_block
    key_parts = gathered[:, 0].reshape(block_count, key_block, group_count, head_width)
    value_parts = gathered[:, 1].reshape(block_count, key_block, group_count, head_width)
    spot_parts = all_spots.reshape(block_count, key_block)

    def forward_step(loop_carry, block_data):
        row_total, summed = loop_carry
        keys_part, values_part, key_spot = block_data
        exp_score, bent_score = score_block(queries_b, keys_part, own_spots, key_spot, score_scale)
        row_total = row_total + jnp.sum(exp_score, axis=-1)
        summed = summed + jnp.einsum(
            "gjqk,kgd->qgjd",
            exp_score.astype(jnp.bfloat16),
            values_part,
            preferred_element_type=jnp.float32,
        )
        return ((row_total, summed), None)

    start_total = jnp.zeros((group_count, pair_count, tok_rows), jnp.float32)
    start_summed = jnp.zeros((tok_rows, group_count, pair_count, head_width), jnp.float32)
    (row_total, summed), _ = lax.scan(
        forward_step, (start_total, start_summed), (key_parts, value_parts, spot_parts)
    )
    total_rows = jnp.transpose(row_total, (2, 0, 1))[..., None]
    mixed_b = (summed / total_rows).astype(jnp.bfloat16).reshape(tok_rows, -1)
    attend_part = lax.dot_general(
        mixed_b, output_full, CONTRACT_LAST, preferred_element_type=jnp.float32
    )
    attend_sum = lax.psum(attend_part, "head")
    first_sum = hidden + norm_apply(attend_sum, gains_all[1])
    normed_two_b = norm_apply(first_sum, gains_all[2]).astype(jnp.bfloat16)
    gate_up = jnp.dot(normed_two_b, expand_full, preferred_element_type=jnp.float32)
    gate_act = gate_up[:, :hidden_width]
    up_act = gate_up[:, hidden_width:]
    inner_b = gate_product(gate_act, up_act).astype(jnp.bfloat16)
    feed_part = lax.dot_general(
        inner_b, shrink_full, CONTRACT_LAST, preferred_element_type=jnp.float32
    )
    feed_sum = lax.psum(feed_part, "head")
    hidden_out = (first_sum + norm_apply(feed_sum, gains_all[3])).astype(jnp.bfloat16)
    grad_out = out_cotangent.astype(jnp.float32)
    grad_feed, gain_four = norm_back(feed_sum, gains_all[3], grad_out)
    grad_feed_b = grad_feed.astype(jnp.bfloat16)
    grad_inner = jnp.dot(grad_feed_b, shrink_full, preferred_element_type=jnp.float32)
    _, pull_back = jax.vjp(gate_product, gate_act, up_act)
    grad_gate, grad_up = pull_back(grad_inner)
    grad_gate_up_b = jnp.concatenate([grad_gate, grad_up], axis=1).astype(jnp.bfloat16)
    feed_pairs = ((normed_two_b, grad_gate_up_b), (grad_feed_b, inner_b))
    grad_two_part = lax.dot_general(
        grad_gate_up_b, expand_full, CONTRACT_LAST, preferred_element_type=jnp.float32
    )
    grad_two = lax.psum(grad_two_part, "head")
    grad_first_norm, gain_three = norm_back(first_sum, gains_all[2], grad_two)
    grad_first = grad_out + grad_first_norm
    grad_attend, gain_two = norm_back(attend_sum, gains_all[1], grad_first)
    grad_attend_b = grad_attend.astype(jnp.bfloat16)
    grad_mixed = jnp.dot(grad_attend_b, output_full, preferred_element_type=jnp.float32).reshape(
        tok_rows, group_count, pair_count, head_width
    )
    grad_summed_b = (grad_mixed / total_rows).astype(jnp.bfloat16)
    delta_rows = jnp.sum(grad_mixed * summed, axis=-1) / (total_rows[..., 0] * total_rows[..., 0])
    row_delta = jnp.transpose(delta_rows, (1, 2, 0))

    def backward_step(grad_query, block_data):
        keys_part, values_part, key_spot = block_data
        exp_score, bent_score = score_block(queries_b, keys_part, own_spots, key_spot, score_scale)
        grad_exp = (
            jnp.einsum(
                "qgjd,kgd->gjqk", grad_summed_b, values_part, preferred_element_type=jnp.float32
            )
            - row_delta[..., None]
        )
        grad_raw_b = (exp_score * grad_exp * (1.0 - bent_score * bent_score) * score_scale).astype(
            jnp.bfloat16
        )
        grad_query = grad_query + jnp.einsum(
            "gjqk,kgd->qgjd", grad_raw_b, keys_part, preferred_element_type=jnp.float32
        )
        grad_key = jnp.einsum(
            "gjqk,qgjd->kgd", grad_raw_b, queries_b, preferred_element_type=jnp.float32
        )
        grad_value = jnp.einsum(
            "gjqk,qgjd->kgd",
            exp_score.astype(jnp.bfloat16),
            grad_summed_b,
            preferred_element_type=jnp.float32,
        )
        return (grad_query, jnp.stack([grad_key, grad_value], axis=1))

    start_query = jnp.zeros((tok_rows, group_count, pair_count, head_width), jnp.float32)
    grad_query, key_terms = lax.scan(
        backward_step, start_query, (key_parts, value_parts, spot_parts)
    )
    own_key_grads = lax.psum_scatter(
        key_terms.reshape(length, -1), "ctx", scatter_dimension=0, tiled=True
    ).reshape(tok_rows, 2, group_count, head_width)
    grad_query_pre = rotate(grad_query, cosine[:, None, None], -sine_table[:, None, None])
    grad_key_pre = rotate(own_key_grads[:, 0], cosine[:, None], -sine_table[:, None])
    grad_proj_b = (
        jnp.concatenate(
            [grad_query_pre, grad_key_pre[:, :, None], own_key_grads[:, 1][:, :, None]], axis=2
        )
        .astype(jnp.bfloat16)
        .reshape(tok_rows, -1)
    )
    grad_normed_part = lax.dot_general(
        grad_proj_b, attend_full, CONTRACT_LAST, preferred_element_type=jnp.float32
    )
    grad_normed = lax.psum(grad_normed_part.astype(jnp.bfloat16), "head").astype(jnp.float32)
    grad_hidden_norm, gain_one = norm_back(hidden, gains_all[0], grad_normed)
    hidden_grad = grad_first + grad_hidden_norm
    attend_pairs = ((normed_b, grad_proj_b), (grad_attend_b, mixed_b))
    attend_cols = group_count * slot_count * head_width
    output_cols = mixed_b.shape[1]
    every_grad = column_sums(attend_pairs + feed_pairs, local_width, block_cols, send_all)
    attend_grads = every_grad[:, : attend_cols + output_cols]
    feed_grads = every_grad[:, attend_cols + output_cols :]
    gains_grad = lax.psum_scatter(
        jnp.stack([gain_one, gain_two, gain_three, gain_four]),
        "ctx",
        scatter_dimension=1,
        tiled=True,
    )
    expand_cols = 2 * hidden_width
    attend_grad = attend_grads[:, :attend_cols].reshape(attend_weight.shape)
    output_grad = attend_grads[:, attend_cols:].T.reshape(output_weight.shape)
    expand_grad = feed_grads[:, :expand_cols].reshape(expand_weight.shape)
    shrink_grad = feed_grads[:, expand_cols:].T
    attend_after, attend_mean, attend_power = adam_step(
        attend_weight, attend_moment, attend_square, attend_grad, RATE_MATRIX, DECAY
    )
    output_after, output_mean, output_power = adam_step(
        output_weight, output_moment, output_square, output_grad, RATE_MATRIX, DECAY
    )
    expand_after, expand_mean, expand_power = adam_step(
        expand_weight, expand_moment, expand_square, expand_grad, RATE_MATRIX, DECAY
    )
    shrink_after, shrink_mean, shrink_power = adam_step(
        shrink_weight, shrink_moment, shrink_square, shrink_grad, RATE_MATRIX, DECAY
    )
    gains_after, gains_mean, gains_power = adam_step(
        gains_weight, gains_moment, gains_square, gains_grad, RATE_GAIN, 0.0
    )
    return (
        hidden_out,
        hidden_grad,
        attend_grad,
        attend_after,
        attend_mean,
        attend_power,
        output_grad,
        output_after,
        output_mean,
        output_power,
        expand_grad,
        expand_after,
        expand_mean,
        expand_power,
        shrink_grad,
        shrink_after,
        shrink_mean,
        shrink_power,
        gains_grad,
        gains_after,
        gains_mean,
        gains_power,
    )


def solution(mesh):
    in_specs = (
        P("ctx", None),
        P("ctx", None),
        P(),
        P("ctx", "head", None, None),
        P("ctx", "head", None, None),
        P("ctx", "head", None, None),
        P("head", None, "ctx"),
        P("head", None, "ctx"),
        P("head", None, "ctx"),
        P("ctx", None, "head"),
        P("ctx", None, "head"),
        P("ctx", None, "head"),
        P("head", "ctx"),
        P("head", "ctx"),
        P("head", "ctx"),
        P(None, "ctx"),
        P(None, "ctx"),
        P(None, "ctx"),
    )
    out_specs = (
        P("ctx", None),
        P("ctx", None),
        P("ctx", "head", None, None),
        P("ctx", "head", None, None),
        P("ctx", "head", None, None),
        P("ctx", "head", None, None),
        P("head", None, "ctx"),
        P("head", None, "ctx"),
        P("head", None, "ctx"),
        P("head", None, "ctx"),
        P("ctx", None, "head"),
        P("ctx", None, "head"),
        P("ctx", None, "head"),
        P("ctx", None, "head"),
        P("head", "ctx"),
        P("head", "ctx"),
        P("head", "ctx"),
        P("head", "ctx"),
        P(None, "ctx"),
        P(None, "ctx"),
        P(None, "ctx"),
        P(None, "ctx"),
    )
    return jax.shard_map(body, mesh=mesh, in_specs=in_specs, out_specs=out_specs, check_vma=False)
```

profile of v0, /device:TPU:0, one launch (start us, length us, event | category | flops | bytes accessed | tf_op | source)
XLA Modules:
  0.0 3486.4 jit_solution(17014010799100026016)
XLA Ops:
  55.9 80.8 %all-gather.7.cloned.1.call-done = bf16[2304,2048]{1,0:T(8,128)(2,1)} async-done(((bf16[144,2048]{1,0:T(8,128)(2,1)}), bf16[2304,2048]{1,0:T(8,128)(2,1)}) %all-gather.7.cloned.1.call-update) | async-done | bytes 9437200 | tf_op jit(solution)/shard_map/all_gather | solution.py:161
  149.2 85.9 %all-gather.9.cloned.1.call-done = bf16[2048,1024]{0,1:T(8,128)(2,1)} async-done(((bf16[128,1024]{0,1:T(8,128)(2,1)}), bf16[2048,1024]{0,1:T(8,128)(2,1)}) %all-gather.9.cloned.1.call-update) | async-done | bytes 4194320 | tf_op jit(solution)/shard_map/all_gather | solution.py:182
  242.2 75.0 %all-gather.11.cloned.1.call-done = bf16[2304,1024]{1,0:T(8,128)(2,1)} async-done(((bf16[144,1024]{1,0:T(8,128)(2,1)}), bf16[2304,1024]{1,0:T(8,128)(2,1)}) %all-gather.11.cloned.1.call-update) | async-done | bytes 4718608 | tf_op jit(solution)/shard_map/all_gather | solution.py:162
  345.4 435.3 %all-gather.13.cloned.1.call-done = bf16[2304,9216]{1,0:T(8,128)(2,1)} async-done(((bf16[144,9216]{1,0:T(8,128)(2,1)}), bf16[2304,9216]{1,0:T(8,128)(2,1)}) %all-gather.13.cloned.1.call-update) | async-done | bytes 42467344 | tf_op jit(solution)/shard_map/all_gather | solution.py:163
  803.2 213.2 %all-gather.15.cloned.1.call-done = bf16[2304,4608]{1,0:T(8,128)(2,1)} async-done(((bf16[144,4608]{1,0:T(8,128)(2,1)}), bf16[2304,4608]{1,0:T(8,128)(2,1)}) %all-gather.15.cloned.1.call-update) | async-done | bytes 21233680 | tf_op jit(solution)/shard_map/all_gather | solution.py:164
  1131.0 1206.2 %while.64 = (s32[]{:T(128)}, f32[144,9216]{1,0:T(8,128)}, bf16[128,9216]{1,0:T(8,128)(2,1)}, bf16[128,2304]{1,0:T(8,128)(2,1)S(1)}, s32[]{:T(128)}, /*index=5*/s32[]{:T(128)}, s32[]{:T(128)}, s32[]{:T(128)}) while((s32[]{:T(128)}, f32[144,9216]{1,0:T(8,128)}, bf16[128,9216]{1,0:T(8,128)(2,1)}, bf16[128,2304]{1,0:T(8,128)(2,1)S(1)}, ...), condition=%wide.region_23.24_spmd, body=%wide.region_21.23_spmd.sunk | while | flops 305455104 | bytes 18120876 | solution.py:105
  1141.9 65.0 %all-to-all-done.2 = bf16[16,144,512]{2,1,0:T(8,128)(2,1)S(1)} async-done(((bf16[16,144,512]{2,1,0:T(8,128)(2,1)}), bf16[16,144,512]{2,1,0:T(8,128)(2,1)S(1)}, u32[]{:S(2)}, u32[]{:S(2)}) %all-to-all-start.2) | async-done | bytes 2359328 | tf_op jit(solution)/shard_map/while/body/eval_jaxpr/all_to_all | solution.py:145
  1239.0 56.3 %all-to-all-done.2 = bf16[16,144,512]{2,1,0:T(8,128)(2,1)S(1)} async-done(((bf16[16,144,512]{2,1,0:T(8,128)(2,1)}), bf16[16,144,512]{2,1,0:T(8,128)(2,1)S(1)}, u32[]{:S(2)}, u32[]{:S(2)}) %all-to-all-start.2) | async-done | bytes 2359328 | tf_op jit(solution)/shard_map/while/body/eval_jaxpr/all_to_all | solution.py:145
  1326.9 61.1 %all-to-all-done.2 = bf16[16,144,512]{2,1,0:T(8,128)(2,1)S(1)} async-done(((bf16[16,144,512]{2,1,0:T(8,128)(2,1)}), bf16[16,144,512]{2,1,0:T(8,128)(2,1)S(1)}, u32[]{:S(2)}, u32[]{:S(2)}) %all-to-all-start.2) | async-done | bytes 2359328 | tf_op jit(solution)/shard_map/while/body/eval_jaxpr/all_to_all | solution.py:145
  1469.7 47.0 %all-to-all-done.2 = bf16[16,144,512]{2,1,0:T(8,128)(2,1)S(1)} async-done(((bf16[16,144,512]{2,1,0:T(8,128)(2,1)}), bf16[16,144,512]{2,1,0:T(8,128)(2,1)S(1)}, u32[]{:S(2)}, u32[]{:S(2)}) %all-to-all-start.2) | async-done | bytes 2359328 | tf_op jit(solution)/shard_map/while/body/eval_jaxpr/all_to_all | solution.py:145
  1532.8 47.0 %all-to-all-done.2 = bf16[16,144,512]{2,1,0:T(8,128)(2,1)S(1)} async-done(((bf16[16,144,512]{2,1,0:T(8,128)(2,1)}), bf16[16,144,512]{2,1,0:T(8,128)(2,1)S(1)}, u32[]{:S(2)}, u32[]{:S(2)}) %all-to-all-start.2) | async-done | bytes 2359328 | tf_op jit(solution)/shard_map/while/body/eval_jaxpr/all_to_all | solution.py:145
  1595.8 47.0 %all-to-all-done.2 = bf16[16,144,512]{2,1,0:T(8,128)(2,1)S(1)} async-done(((bf16[16,144,512]{2,1,0:T(8,128)(2,1)}), bf16[16,144,512]{2,1,0:T(8,128)(2,1)S(1)}, u32[]{:S(2)}, u32[]{:S(2)}) %all-to-all-start.2) | async-done | bytes 2359328 | tf_op jit(solution)/shard_map/while/body/eval_jaxpr/all_to_all | solution.py:145
  1658.8 47.0 %all-to-all-done.2 = bf16[16,144,512]{2,1,0:T(8,128)(2,1)S(1)} async-done(((bf16[16,144,512]{2,1,0:T(8,128)(2,1)}), bf16[16,144,512]{2,1,0:T(8,128)(2,1)S(1)}, u32[]{:S(2)}, u32[]{:S(2)}) %all-to-all-start.2) | async-done | bytes 2359328 | tf_op jit(solution)/shard_map/while/body/eval_jaxpr/all_to_all | solution.py:145
  1721.9 47.0 %all-to-all-done.2 = bf16[16,144,512]{2,1,0:T(8,128)(2,1)S(1)} async-done(((bf16[16,144,512]{2,1,0:T(8,128)(2,1)}), bf16[16,144,512]{2,1,0:T(8,128)(2,1)S(1)}, u32[]{:S(2)}, u32[]{:S(2)}) %all-to-all-start.2) | async-done | bytes 2359328 | tf_op jit(solution)/shard_map/while/body/eval_jaxpr/all_to_all | solution.py:145
  1784.9 47.0 %all-to-all-done.2 = bf16[16,144,512]{2,1,0:T(8,128)(2,1)S(1)} async-done(((bf16[16,144,512]{2,1,0:T(8,128)(2,1)}), bf16[16,144,512]{2,1,0:T(8,128)(2,1)S(1)}, u32[]{:S(2)}, u32[]{:S(2)}) %all-to-all-start.2) | async-done | bytes 2359328 | tf_op jit(solution)/shard_map/while/body/eval_jaxpr/all_to_all | solution.py:145
  1847.9 47.0 %all-to-all-done.2 = bf16[16,144,512]{2,1,0:T(8,128)(2,1)S(1)} async-done(((bf16[16,144,512]{2,1,0:T(8,128)(2,1)}), bf16[16,144,512]{2,1,0:T(8,128)(2,1)S(1)}, u32[]{:S(2)}, u32[]{:S(2)}) %all-to-all-start.2) | async-done | bytes 2359328 | tf_op jit(solution)/shard_map/while/body/eval_jaxpr/all_to_all | solution.py:145
  1911.0 47.0 %all-to-all-done.2 = bf16[16,144,512]{2,1,0:T(8,128)(2,1)S(1)} async-done(((bf16[16,144,512]{2,1,0:T(8,128)(2,1)}), bf16[16,144,512]{2,1,0:T(8,128)(2,1)S(1)}, u32[]{:S(2)}, u32[]{:S(2)}) %all-to-all-start.2) | async-done | bytes 2359328 | tf_op jit(solution)/shard_map/while/body/eval_jaxpr/all_to_all | solution.py:145
  2037.0 47.0 %all-to-all-done.2 = bf16[16,144,512]{2,1,0:T(8,128)(2,1)S(1)} async-done(((bf16[16,144,512]{2,1,0:T(8,128)(2,1)}), bf16[16,144,512]{2,1,0:T(8,128)(2,1)S(1)}, u32[]{:S(2)}, u32[]{:S(2)}) %all-to-all-start.2) | async-done | bytes 2359328 | tf_op jit(solution)/shard_map/while/body/eval_jaxpr/all_to_all | solution.py:145
  2163.1 47.0 %all-to-all-done.2 = bf16[16,144,512]{2,1,0:T(8,128)(2,1)S(1)} async-done(((bf16[16,144,512]{2,1,0:T(8,128)(2,1)}), bf16[16,144,512]{2,1,0:T(8,128)(2,1)S(1)}, u32[]{:S(2)}, u32[]{:S(2)}) %all-to-all-start.2) | async-done | bytes 2359328 | tf_op jit(solution)/shard_map/while/body/eval_jaxpr/all_to_all | solution.py:145
  2289.1 47.0 %all-to-all-done.2 = bf16[16,144,512]{2,1,0:T(8,128)(2,1)S(1)} async-done(((bf16[16,144,512]{2,1,0:T(8,128)(2,1)}), bf16[16,144,512]{2,1,0:T(8,128)(2,1)S(1)}, u32[]{:S(2)}, u32[]{:S(2)}) %all-to-all-start.2) | async-done | bytes 2359328 | tf_op jit(solution)/shard_map/while/body/eval_jaxpr/all_to_all | solution.py:145
  2346.9 567.3 %while.65 = (s32[]{:T(128)}, f32[144,4608]{1,0:T(8,128)}, bf16[128,4608]{1,0:T(8,128)(2,1)}, bf16[128,2304]{1,0:T(8,128)(2,1)S(1)}, s32[]{:T(128)}, /*index=5*/s32[]{:T(128)}, s32[]{:T(128)}, s32[]{:T(128)}) while((s32[]{:T(128)}, f32[144,4608]{1,0:T(8,128)}, bf16[128,4608]{1,0:T(8,128)(2,1)}, bf16[128,2304]{1,0:T(8,128)(2,1)S(1)}, ...), condition=%wide.region_26.27_spmd, body=%wide.region_24.26_spmd.sunk | while | flops 305455104 | bytes 18120876 | solution.py:105
  2361.9 47.0 %all-to-all-done.3 = bf16[16,144,512]{2,1,0:T(8,128)(2,1)S(1)} async-done(((bf16[16,144,512]{2,1,0:T(8,128)(2,1)}), bf16[16,144,512]{2,1,0:T(8,128)(2,1)S(1)}, u32[]{:S(2)}, u32[]{:S(2)}) %all-to-all-start.3) | async-done | bytes 2359328 | tf_op jit(solution)/shard_map/while/body/eval_jaxpr/all_to_all | solution.py:145
  2424.9 47.0 %all-to-all-done.3 = bf16[16,144,512]{2,1,0:T(8,128)(2,1)S(1)} async-done(((bf16[16,144,512]{2,1,0:T(8,128)(2,1)}), bf16[16,144,512]{2,1,0:T(8,128)(2,1)S(1)}, u32[]{:S(2)}, u32[]{:S(2)}) %all-to-all-start.3) | async-done | bytes 2359328 | tf_op jit(solution)/shard_map/while/body/eval_jaxpr/all_to_all | solution.py:145
  2487.9 47.0 %all-to-all-done.3 = bf16[16,144,512]{2,1,0:T(8,128)(2,1)S(1)} async-done(((bf16[16,144,512]{2,1,0:T(8,128)(2,1)}), bf16[16,144,512]{2,1,0:T(8,128)(2,1)S(1)}, u32[]{:S(2)}, u32[]{:S(2)}) %all-to-all-start.3) | async-done | bytes 2359328 | tf_op jit(solution)/shard_map/while/body/eval_jaxpr/all_to_all | solution.py:145
  2614.0 47.0 %all-to-all-done.3 = bf16[16,144,512]{2,1,0:T(8,128)(2,1)S(1)} async-done(((bf16[16,144,512]{2,1,0:T(8,128)(2,1)}), bf16[16,144,512]{2,1,0:T(8,128)(2,1)S(1)}, u32[]{:S(2)}, u32[]{:S(2)}) %all-to-all-start.3) | async-done | bytes 2359328 | tf_op jit(solution)/shard_map/while/body/eval_jaxpr/all_to_all | solution.py:145
  2740.1 47.0 %all-to-all-done.3 = bf16[16,144,512]{2,1,0:T(8,128)(2,1)S(1)} async-done(((bf16[16,144,512]{2,1,0:T(8,128)(2,1)}), bf16[16,144,512]{2,1,0:T(8,128)(2,1)S(1)}, u32[]{:S(2)}, u32[]{:S(2)}) %all-to-all-start.3) | async-done | bytes 2359328 | tf_op jit(solution)/shard_map/while/body/eval_jaxpr/all_to_all | solution.py:145
  2866.1 47.0 %all-to-all-done.3 = bf16[16,144,512]{2,1,0:T(8,128)(2,1)S(1)} async-done(((bf16[16,144,512]{2,1,0:T(8,128)(2,1)}), bf16[16,144,512]{2,1,0:T(8,128)(2,1)S(1)}, u32[]{:S(2)}, u32[]{:S(2)}) %all-to-all-start.3) | async-done | bytes 2359328 | tf_op jit(solution)/shard_map/while/body/eval_jaxpr/all_to_all | solution.py:145
  2947.9 125.9 %while.63 = (s32[]{:T(128)}, f32[144,1024]{1,0:T(8,128)}, bf16[128,1024]{0,1:T(8,128)(2,1)S(1)}, bf16[128,2304]{1,0:T(8,128)(2,1)S(1)}, s32[]{:T(128)}, /*index=5*/s32[]{:T(128)}, s32[]{:T(128)}, s32[]{:T(128)}) while((s32[]{:T(128)}, f32[144,1024]{1,0:T(8,128)}, bf16[128,1024]{0,1:T(8,128)(2,1)S(1)}, bf16[128,2304]{1,0:T(8,128)(2,1)S(1)}, ...), condition=%wide.region_20.21_spmd, body=%wide.region_18.20_spmd.sunk | while | flops 305455104 | bytes 22839524 | solution.py:105
  2962.0 47.0 %all-to-all-done.1 = bf16[16,144,512]{2,1,0:T(8,128)(2,1)S(1)} async-done(((bf16[16,144,512]{2,1,0:T(8,128)(2,1)}), bf16[16,144,512]{2,1,0:T(8,128)(2,1)S(1)}, u32[]{:S(2)}, u32[]{:S(2)}) %all-to-all-start.1) | async-done | bytes 2359328 | tf_op jit(solution)/shard_map/while/body/eval_jaxpr/all_to_all | solution.py:145
  3024.9 47.0 %all-to-all-done.1 = bf16[16,144,512]{2,1,0:T(8,128)(2,1)S(1)} async-done(((bf16[16,144,512]{2,1,0:T(8,128)(2,1)}), bf16[16,144,512]{2,1,0:T(8,128)(2,1)S(1)}, u32[]{:S(2)}, u32[]{:S(2)}) %all-to-all-start.1) | async-done | bytes 2359328 | tf_op jit(solution)/shard_map/while/body/eval_jaxpr/all_to_all | solution.py:145
  3088.7 248.7 %while.62 = (s32[]{:T(128)}, f32[144,2048]{1,0:T(8,128)}, bf16[128,2048]{0,1:T(8,128)(2,1)S(1)}, bf16[128,2304]{1,0:T(8,128)(2,1)S(1)}, s32[]{:T(128)}, /*index=5*/s32[]{:T(128)}, s32[]{:T(128)}, s32[]{:T(128)}) while((s32[]{:T(128)}, f32[144,2048]{1,0:T(8,128)}, bf16[128,2048]{0,1:T(8,128)(2,1)S(1)}, bf16[128,2304]{1,0:T(8,128)(2,1)S(1)}, ...), condition=%wide.region_17.18_spmd, body=%wide.region_15.17_spmd.sunk | while | flops 305455104 | bytes 18120876 | solution.py:105
  3349.9 128.2 %reduce-scatter.7.cloned.1.call-done = f32[144,4]{1,0:T(8,128)} async-done(((f32[2304,4]{1,0:T(8,128)}), f32[144,4]{1,0:T(8,128)}) %reduce-scatter.7.cloned.1.call-update) | async-done | bytes 2320
  (433 shorter events, 1376.8 us)
Async XLA Ops:
  7.2 129.5 %all-gather.7.cloned.1.call-start = ((), (), s32[]{:S(2)}) async-start(), calls=%async_computation.6 | async-start | bytes 10027008 | tf_op jit(solution)/shard_map/all_gather | solution.py:161
  10.1 225.0 %all-gather.9.cloned.1.call-start = ((), (), s32[]{:S(2)}) async-start(), calls=%async_computation.7 | async-start | bytes 4456448 | tf_op jit(solution)/shard_map/all_gather | solution.py:182
  147.6 169.6 %all-gather.11.cloned.1.call-start = ((), (), s32[]{:S(2)}) async-start(), calls=%async_computation.8 | async-start | bytes 5013504 | tf_op jit(solution)/shard_map/all_gather | solution.py:162
  148.4 193.7 %all-reduce.5.cloned.1.call-start = ((), (), s32[]{:S(2)}) async-start(), calls=%async_computation.9 | async-start | bytes 2359296 | tf_op jit(solution)/shard_map/psum | solution.py:214
  322.2 458.4 %all-gather.13.cloned.1.call-start = ((), (), s32[]{:S(2)}) async-start(), calls=%async_computation.10 | async-start | bytes 45121536 | tf_op jit(solution)/shard_map/all_gather | solution.py:163
  328.5 688.0 %all-gather.15.cloned.1.call-start = ((), (), s32[]{:S(2)}) async-start(), calls=%async_computation.11 | async-start | bytes 22560768 | tf_op jit(solution)/shard_map/all_gather | solution.py:164
  331.7 715.0 %all-reduce.7.cloned.1.call-start = ((), (), s32[]{:S(2)}) async-start(), calls=%async_computation.12 | async-start | bytes 2359296 | tf_op jit(solution)/shard_map/psum | solution.py:224
  1028.5 79.0 %all-reduce.9.cloned.1.call-start = ((), (), s32[]{:S(2)}) async-start(), calls=%async_computation.13 | async-start | bytes 2359296 | tf_op jit(solution)/shard_map/psum | solution.py:237
  1086.4 1990.5 %reduce-scatter.5.cloned.1.call-start = ((), (), s32[]{:S(2)}) async-start(), calls=%async_computation.14 | async-start | bytes 8912896 | tf_op jit(solution)/shard_map/reduce_scatter | solution.py:279
  1127.6 2217.6 %all-reduce.11.cloned.1.call-start = ((), (), s32[]{:S(2)}) async-start(), calls=%async_computation.15 | async-start | bytes 1179648 | tf_op jit(solution)/shard_map/psum | solution.py:294
  1135.1 71.8 %all-to-all-start.2 = ((bf16[16,144,512]{2,1,0:T(8,128)(2,1)}), bf16[16,144,512]{2,1,0:T(8,128)(2,1)S(1)}, u32[]{:S(2)}, u32[]{:S(2)}) async-start(bf16[16,144,512]{2,1,0:T(8,128)(2,1)} %bitcast.183), calls=%async_computation.2 | async-start | bytes 4718592 | tf_op jit(solution)/shard_map/while/body/eval_jaxpr/all_to_all | solution.py:145
  1212.2 83.1 %all-to-all-start.2 = ((bf16[16,144,512]{2,1,0:T(8,128)(2,1)}), bf16[16,144,512]{2,1,0:T(8,128)(2,1)S(1)}, u32[]{:S(2)}, u32[]{:S(2)}) async-start(bf16[16,144,512]{2,1,0:T(8,128)(2,1)} %bitcast.183), calls=%async_computation.2 | async-start | bytes 4718592 | tf_op jit(solution)/shard_map/while/body/eval_jaxpr/all_to_all | solution.py:145
  1300.5 87.5 %all-to-all-start.2 = ((bf16[16,144,512]{2,1,0:T(8,128)(2,1)}), bf16[16,144,512]{2,1,0:T(8,128)(2,1)S(1)}, u32[]{:S(2)}, u32[]{:S(2)}) async-start(bf16[16,144,512]{2,1,0:T(8,128)(2,1)} %bitcast.183), calls=%async_computation.2 | async-start | bytes 4718592 | tf_op jit(solution)/shard_map/while/body/eval_jaxpr/all_to_all | solution.py:145
  1393.2 60.5 %all-to-all-start.2 = ((bf16[16,144,512]{2,1,0:T(8,128)(2,1)}), bf16[16,144,512]{2,1,0:T(8,128)(2,1)S(1)}, u32[]{:S(2)}, u32[]{:S(2)}) async-start(bf16[16,144,512]{2,1,0:T(8,128)(2,1)} %bitcast.183), calls=%async_computation.2 | async-start | bytes 4718592 | tf_op jit(solution)/shard_map/while/body/eval_jaxpr/all_to_all | solution.py:145
  1458.9 57.8 %all-to-all-start.2 = ((bf16[16,144,512]{2,1,0:T(8,128)(2,1)}), bf16[16,144,512]{2,1,0:T(8,128)(2,1)S(1)}, u32[]{:S(2)}, u32[]{:S(2)}) async-start(bf16[16,144,512]{2,1,0:T(8,128)(2,1)} %bitcast.183), calls=%async_computation.2 | async-start | bytes 4718592 | tf_op jit(solution)/shard_map/while/body/eval_jaxpr/all_to_all | solution.py:145
  1521.9 57.8 %all-to-all-start.2 = ((bf16[16,144,512]{2,1,0:T(8,128)(2,1)}), bf16[16,144,512]{2,1,0:T(8,128)(2,1)S(1)}, u32[]{:S(2)}, u32[]{:S(2)}) async-start(bf16[16,144,512]{2,1,0:T(8,128)(2,1)} %bitcast.183), calls=%async_computation.2 | async-start | bytes 4718592 | tf_op jit(solution)/shard_map/while/body/eval_jaxpr/all_to_all | solution.py:145
  1585.0 57.8 %all-to-all-start.2 = ((bf16[16,144,512]{2,1,0:T(8,128)(2,1)}), bf16[16,144,512]{2,1,0:T(8,128)(2,1)S(1)}, u32[]{:S(2)}, u32[]{:S(2)}) async-start(bf16[16,144,512]{2,1,0:T(8,128)(2,1)} %bitcast.183), calls=%async_computation.2 | async-start | bytes 4718592 | tf_op jit(solution)/shard_map/while/body/eval_jaxpr/all_to_all | solution.py:145
  1648.0 57.8 %all-to-all-start.2 = ((bf16[16,144,512]{2,1,0:T(8,128)(2,1)}), bf16[16,144,512]{2,1,0:T(8,128)(2,1)S(1)}, u32[]{:S(2)}, u32[]{:S(2)}) async-start(bf16[16,144,512]{2,1,0:T(8,128)(2,1)} %bitcast.183), calls=%async_computation.2 | async-start | bytes 4718592 | tf_op jit(solution)/shard_map/while/body/eval_jaxpr/all_to_all | solution.py:145
  1774.1 57.8 %all-to-all-start.2 = ((bf16[16,144,512]{2,1,0:T(8,128)(2,1)}), bf16[16,144,512]{2,1,0:T(8,128)(2,1)S(1)}, u32[]{:S(2)}, u32[]{:S(2)}) async-start(bf16[16,144,512]{2,1,0:T(8,128)(2,1)} %bitcast.183), calls=%async_computation.2 | async-start | bytes 4718592 | tf_op jit(solution)/shard_map/while/body/eval_jaxpr/all_to_all | solution.py:145
  1900.1 57.8 %all-to-all-start.2 = ((bf16[16,144,512]{2,1,0:T(8,128)(2,1)}), bf16[16,144,512]{2,1,0:T(8,128)(2,1)S(1)}, u32[]{:S(2)}, u32[]{:S(2)}) async-start(bf16[16,144,512]{2,1,0:T(8,128)(2,1)} %bitcast.183), calls=%async_computation.2 | async-start | bytes 4718592 | tf_op jit(solution)/shard_map/while/body/eval_jaxpr/all_to_all | solution.py:145
  2026.2 57.8 %all-to-all-start.2 = ((bf16[16,144,512]{2,1,0:T(8,128)(2,1)}), bf16[16,144,512]{2,1,0:T(8,128)(2,1)S(1)}, u32[]{:S(2)}, u32[]{:S(2)}) async-start(bf16[16,144,512]{2,1,0:T(8,128)(2,1)} %bitcast.183), calls=%async_computation.2 | async-start | bytes 4718592 | tf_op jit(solution)/shard_map/while/body/eval_jaxpr/all_to_all | solution.py:145
  2152.3 57.8 %all-to-all-start.2 = ((bf16[16,144,512]{2,1,0:T(8,128)(2,1)}), bf16[16,144,512]{2,1,0:T(8,128)(2,1)S(1)}, u32[]{:S(2)}, u32[]{:S(2)}) async-start(bf16[16,144,512]{2,1,0:T(8,128)(2,1)} %bitcast.183), calls=%async_computation.2 | async-start | bytes 4718592 | tf_op jit(solution)/shard_map/while/body/eval_jaxpr/all_to_all | solution.py:145
  2278.3 57.8 %all-to-all-start.2 = ((bf16[16,144,512]{2,1,0:T(8,128)(2,1)}), bf16[16,144,512]{2,1,0:T(8,128)(2,1)S(1)}, u32[]{:S(2)}, u32[]{:S(2)}) async-start(bf16[16,144,512]{2,1,0:T(8,128)(2,1)} %bitcast.183), calls=%async_computation.2 | async-start | bytes 4718592 | tf_op jit(solution)/shard_map/while/body/eval_jaxpr/all_to_all | solution.py:145
  2351.1 57.8 %all-to-all-start.3 = ((bf16[16,144,512]{2,1,0:T(8,128)(2,1)}), bf16[16,144,512]{2,1,0:T(8,128)(2,1)S(1)}, u32[]{:S(2)}, u32[]{:S(2)}) async-start(bf16[16,144,512]{2,1,0:T(8,128)(2,1)} %bitcast.184), calls=%async_computation.3 | async-start | bytes 4718592 | tf_op jit(solution)/shard_map/while/body/eval_jaxpr/all_to_all | solution.py:145
  2414.1 57.8 %all-to-all-start.3 = ((bf16[16,144,512]{2,1,0:T(8,128)(2,1)}), bf16[16,144,512]{2,1,0:T(8,128)(2,1)S(1)}, u32[]{:S(2)}, u32[]{:S(2)}) async-start(bf16[16,144,512]{2,1,0:T(8,128)(2,1)} %bitcast.184), calls=%async_computation.3 | async-start | bytes 4718592 | tf_op jit(solution)/shard_map/while/body/eval_jaxpr/all_to_all | solution.py:145
  2477.1 57.8 %all-to-all-start.3 = ((bf16[16,144,512]{2,1,0:T(8,128)(2,1)}), bf16[16,144,512]{2,1,0:T(8,128)(2,1)S(1)}, u32[]{:S(2)}, u32[]{:S(2)}) async-start(bf16[16,144,512]{2,1,0:T(8,128)(2,1)} %bitcast.184), calls=%async_computation.3 | async-start | bytes 4718592 | tf_op jit(solution)/shard_map/while/body/eval_jaxpr/all_to_all | solution.py:145
  2603.2 57.8 %all-to-all-start.3 = ((bf16[16,144,512]{2,1,0:T(8,128)(2,1)}), bf16[16,144,512]{2,1,0:T(8,128)(2,1)S(1)}, u32[]{:S(2)}, u32[]{:S(2)}) async-start(bf16[16,144,512]{2,1,0:T(8,128)(2,1)} %bitcast.184), calls=%async_computation.3 | async-start | bytes 4718592 | tf_op jit(solution)/shard_map/while/body/eval_jaxpr/all_to_all | solution.py:145
  2729.3 57.8 %all-to-all-start.3 = ((bf16[16,144,512]{2,1,0:T(8,128)(2,1)}), bf16[16,144,512]{2,1,0:T(8,128)(2,1)S(1)}, u32[]{:S(2)}, u32[]{:S(2)}) async-start(bf16[16,144,512]{2,1,0:T(8,128)(2,1)} %bitcast.184), calls=%async_computation.3 | async-start | bytes 4718592 | tf_op jit(solution)/shard_map/while/body/eval_jaxpr/all_to_all | solution.py:145
  2855.3 57.8 %all-to-all-start.3 = ((bf16[16,144,512]{2,1,0:T(8,128)(2,1)}), bf16[16,144,512]{2,1,0:T(8,128)(2,1)S(1)}, u32[]{:S(2)}, u32[]{:S(2)}) async-start(bf16[16,144,512]{2,1,0:T(8,128)(2,1)} %bitcast.184), calls=%async_computation.3 | async-start | bytes 4718592 | tf_op jit(solution)/shard_map/while/body/eval_jaxpr/all_to_all | solution.py:145
  2951.2 57.8 %all-to-all-start.1 = ((bf16[16,144,512]{2,1,0:T(8,128)(2,1)}), bf16[16,144,512]{2,1,0:T(8,128)(2,1)S(1)}, u32[]{:S(2)}, u32[]{:S(2)}) async-start(bf16[16,144,512]{2,1,0:T(8,128)(2,1)} %bitcast.185), calls=%async_computation.1 | async-start | bytes 4718592 | tf_op jit(solution)/shard_map/while/body/eval_jaxpr/all_to_all | solution.py:145
  3087.5 390.6 %reduce-scatter.7.cloned.1.call-start = ((), (), s32[]{:S(2)}) async-start(), calls=%async_computation.16 | async-start | bytes 1253376
  3092.1 57.8 %all-to-all-start = ((bf16[16,144,512]{2,1,0:T(8,128)(2,1)}), bf16[16,144,512]{2,1,0:T(8,128)(2,1)S(1)}, u32[]{:S(2)}, u32[]{:S(2)}) async-start(bf16[16,144,512]{2,1,0:T(8,128)(2,1)} %bitcast.186), calls=%async_computation | async-start | bytes 4718592 | tf_op jit(solution)/shard_map/while/body/eval_jaxpr/all_to_all | solution.py:145
  (79 other events, 3175.9 us)
Sparse Core Ops, SparseCore 0:
  11.4 125.2 all-gather.6
  147.7 87.3 all-gather.8
  238.5 78.6 all-gather.10
  322.4 18.4 all-reduce.4
  344.4 436.2 all-gather.12
  784.3 232.1 all-gather.14
  1028.7 17.9 all-reduce.6
  1086.5 20.9 all-reduce.8
  1127.7 258.7 reduce-scatter.4
  3087.6 24.0 all-reduce.10
  3348.5 129.5 reduce-scatter.6
where the time goes:
time: 3500 us; the launch traced here: 3490 us
  waiting for transfers between devices  2650 us (76%)
  starting transfers between devices  399 us (11%)
  matrix products  148 us (4%)
  local copies, waits for them, and re-layouts  146 us (4%)
  other arithmetic  87.9 us (3%)
  blocking collectives  43.2 us (1%)
    all_to_all x33, waiting for transfers between devices, send_all(): lax.all_to_all(partial_value.reshape(shard_count, local_width, -1).astype...  1590 us
    all_gather x1, waiting for transfers between devices, body(): lax.all_gather(packed[2], 'ctx', axis=0, tiled=True)  435 us
    all_to_all x33, starting transfers between devices, send_all(): lax.all_to_all(partial_value.reshape(shard_count, local_width, -1).astype...  387 us
    all_gather x1, waiting for transfers between devices, body(): lax.all_gather(packed[3], 'ctx', axis=0, tiled=True)  213 us
    unnamed x12, waiting for transfers between devices  128 us
    all_gather x1, waiting for transfers between devices, body(): lax.all_gather(own_pairs, 'ctx', axis=0, tiled=True)  85.9 us
    convert_element_type x33, local copies, waits for them, and re-layouts, send_all(): partial_value.reshape(shard_count, local_width, -1).astype(jnp.bfloat16)  80.8 us
    all_gather x1, waiting for transfers between devices, body(): lax.all_gather(packed[0], 'ctx', axis=0, tiled=True)  80.8 us
  transfers between devices with their start and end apart: 44, of which 41 were waited for; matrix products, arithmetic and copies ran while one was open for 8% of the time, Pallas kernels for 0%

commit v1 on v0

v1 whole, which is shorter than its diff:
```python
import jax
import jax.numpy as jnp
from jax import lax
from jax.sharding import PartitionSpec as P

STEP = 10


NORM_EPS = 1e-06
SOFT_CAP = 50.0
ROPE_BASE = 10000.0
RATE_MATRIX = 0.02
RATE_GAIN = 0.1
BETA_ONE = 0.9
BETA_TWO = 0.95
ADAM_EPS = 1e-08
DECAY = 0.1
ROWS = (((0,), (0,)), ((), ()))
LAST = (((1,), (1,)), ((), ()))
LINES = 4
F32 = jnp.float32
BF16 = jnp.bfloat16


def rope_tables(positions, head_width):
    exponent = jnp.arange(head_width // 2, dtype=F32) * (2.0 / head_width)
    frequency = ROPE_BASE ** (-exponent)
    angle = positions.astype(F32)[:, None] * frequency[None, :]
    return (jnp.cos(angle), jnp.sin(angle))


def rotate(values, cosine, sine_table):
    middle = values.shape[-1] // 2
    front_half = values[..., :middle]
    back_half = values[..., middle:]
    return jnp.concatenate(
        [
            front_half * cosine - back_half * sine_table,
            back_half * cosine + front_half * sine_table,
        ],
        axis=-1,
    )


def norm_factor(values):
    return lax.rsqrt(jnp.mean(values * values, axis=-1, keepdims=True) + NORM_EPS)


def norm_apply(values, norm_gain):
    return values * norm_factor(values) * (1.0 + norm_gain)


def norm_back(values, norm_gain, grad_out):
    factor = norm_factor(values)
    weighted = grad_out * (1.0 + norm_gain)
    grad_in = factor * weighted - values * factor * factor * factor * jnp.mean(
        values * weighted, axis=-1, keepdims=True
    )
    grad_gain = jnp.sum(grad_out * values * factor, axis=0)
    return (grad_in, grad_gain)


def gate_product(gate_act, up_act):
    return jax.nn.gelu(gate_act, approximate=True) * up_act


def adam_step(weight, moment, square, grad, rate, decay):
    moment_new = BETA_ONE * moment + (1.0 - BETA_ONE) * grad
    square_new = BETA_TWO * square + (1.0 - BETA_TWO) * grad * grad
    mean_hat = moment_new / (1.0 - BETA_ONE**STEP)
    power_hat = square_new / (1.0 - BETA_TWO**STEP)
    updated = weight - rate * (mean_hat / (jnp.sqrt(power_hat) + ADAM_EPS) + decay * weight)
    return (updated, moment_new, square_new)


def pick(array, index):
    return lax.dynamic_index_in_dim(array, index, 0, keepdims=False)


def put(array, part, index, dim=0):
    return lax.dynamic_update_slice_in_dim(array, jnp.expand_dims(part, dim), index, dim)


def mirror(number, bits):
    return sum(((number >> i) & 1) << (bits - 1 - i) for i in range(bits))


class Grid:
    def __init__(self):
        self.count = lax.axis_size("ctx")
        self.plane = self.count // LINES
        self.bits = self.plane.bit_length() - 1
        rank = lax.axis_index("ctx")
        self.line = rank // self.plane
        self.place = rank % self.plane
        self.core = lax.axis_index("head")

    def along(self, value, step):
        pairs = [(i, i ^ (step * self.plane)) for i in range(self.count)]
        return lax.ppermute(value, "ctx", pairs)

    def across(self, value):
        return lax.ppermute(value, "head", [(0, 1), (1, 0)])

    def within(self, value, phase):
        pairs = []
        for i in range(self.count):
            for core in range(2):
                bit = phase if core == 0 else self.bits - 1 - phase
                pairs.append((2 * i + core, 2 * (i ^ (1 << bit)) + core))
        return lax.ppermute(value, ("ctx", "head"), pairs)

    def place_of(self, mask):
        return self.place ^ jnp.where(self.core == 0, mask, mirror(mask, self.bits))

    def line_gather(self, value):
        near = self.along(value, 1)
        far = self.along(value, 3)
        middle = self.along(far, 1)
        return jnp.concatenate([value, near, middle, far], axis=0)

    def token_gather(self, value):
        own = self.line_gather(value)
        return jnp.concatenate([own, self.across(own)], axis=0)

    def token_reduce(self, partial):
        half = partial.shape[0] // 2
        got = self.across(partial[half:].astype(BF16))
        mine = partial[:half] + got.astype(F32)
        rows = half // LINES
        block = [mine[k * rows : (k + 1) * rows] for k in range(LINES)]
        passed = self.along(block[2].astype(BF16), 1)
        near = self.along(block[1].astype(BF16), 1)
        far = self.along((block[3] + passed.astype(F32)).astype(BF16), 3)
        return block[0] + near.astype(F32) + far.astype(F32)

    def line_swap(self, blocks):
        result = jnp.zeros(blocks.shape, blocks.dtype)
        result = put(result, pick(blocks, self.line), self.line)
        for step in (3, 2, 1):
            other = self.line ^ step
            result = put(result, self.along(pick(blocks, other), step), other)
        return result

    def plane_gather(self, own):
        parts = {0: own}
        for phase in range(self.bits):
            for mask in range(1 << phase):
                parts[mask | (1 << phase)] = self.within(parts[mask], phase)
        return parts

    def plane_reduce(self, parts):
        parts = dict(parts)
        for phase in reversed(range(self.bits)):
            for mask in reversed(range(1 << phase)):
                got = self.within(parts[mask | (1 << phase)], phase)
                parts[mask] = (parts[mask].astype(F32) + got.astype(F32)).astype(BF16)
        return parts[0]

    def weight_spread(self, blocks):
        own = self.line_swap(blocks)
        parts = self.plane_gather(own)
        full = jnp.zeros((LINES, self.plane) + own.shape[1:], own.dtype)
        for mask, part in parts.items():
            full = put(full, part, self.place_of(mask), 1)
        return full.reshape(-1, own.shape[-1])

    def weight_return(self, full):
        shaped = full.reshape(LINES, self.plane, -1, full.shape[-1])
        parts = {
            mask: lax.dynamic_index_in_dim(shaped, self.place_of(mask), 1, keepdims=False)
            for mask in range(self.plane)
        }
        return self.line_swap(self.plane_reduce(parts))


def body(
    hidden_in,
    out_cotangent,
    block_table,
    attend_weight,
    attend_moment,
    attend_square,
    output_weight,
    output_moment,
    output_square,
    expand_weight,
    expand_moment,
    expand_square,
    shrink_weight,
    shrink_moment,
    shrink_square,
    gains_weight,
    gains_moment,
    gains_square,
):
    grid = Grid()
    core = grid.core
    half_rows = hidden_in.shape[0] // 2
    local_width, group_count, slot_count, head_width = attend_weight.shape
    hidden_width = expand_weight.shape[2]
    model_width = hidden_in.shape[1]
    quarter = hidden_width // LINES
    score_scale = head_width ** (-0.5)

    own_in = lax.dynamic_slice_in_dim(hidden_in, core * half_rows, half_rows)
    own_out = lax.dynamic_slice_in_dim(out_cotangent, core * half_rows, half_rows)
    all_in = grid.token_gather(own_in)

    attend_pack = (
        attend_weight.astype(BF16)
        .reshape(local_width, group_count, 2, 2, head_width)
        .transpose(3, 1, 0, 2, 4)
        .reshape(2, group_count, local_width, 2 * head_width)
    )
    output_pack = (
        output_weight.astype(BF16)
        .reshape(group_count, 2, head_width, local_width)
        .transpose(1, 0, 3, 2)
    )

    def core_swap(pack):
        mine = pick(pack, core)
        got = grid.across(pick(pack, 1 - core))
        return jnp.where(
            core == 0, jnp.concatenate([mine, got]), jnp.concatenate([got, mine])
        )

    def core_return(blocks):
        halves = blocks.reshape((2, group_count) + blocks.shape[1:])
        mine = pick(halves, core)
        got = grid.across(pick(halves, 1 - core))
        return jnp.where(core == 0, jnp.stack([mine, got]), jnp.stack([got, mine]))

    attend_full = grid.weight_spread(core_swap(attend_pack))
    output_full = grid.weight_spread(core_swap(output_pack))
    expand_blocks = (
        expand_weight.astype(BF16)
        .reshape(local_width, 2, LINES, quarter)
        .transpose(2, 0, 1, 3)
        .reshape(LINES, local_width, 2 * quarter)
    )
    shrink_blocks = (
        shrink_weight.T.astype(BF16).reshape(local_width, LINES, quarter).transpose(1, 0, 2)
    )
    expand_full = grid.weight_spread(expand_blocks)
    shrink_full = grid.weight_spread(shrink_blocks)

    gains_own = gains_weight.astype(BF16).astype(F32)
    gains_line = grid.line_gather(gains_own[None])
    gains_lines = jnp.zeros((LINES,) + gains_own.shape, F32)
    for step in range(LINES):
        gains_lines = put(gains_lines, gains_line[step], grid.line ^ step)
    gains_grid = jnp.zeros((LINES, grid.plane) + gains_own.shape, F32)
    for mask, part in grid.plane_gather(gains_lines).items():
        gains_grid = put(gains_grid, part, grid.place_of(mask), 1)
    gains_all = gains_grid.transpose(2, 0, 1, 3).reshape(gains_own.shape[0], model_width)

    lines = grid.line ^ jnp.arange(LINES)
    cores = core ^ jnp.arange(2)
    table = block_table.reshape(LINES, grid.plane, 2)
    offsets = jnp.arange(half_rows, dtype=jnp.int32)
    line_table = jnp.take(jnp.take(table, lines, axis=0), cores, axis=2)
    all_spots = (
        line_table.transpose(1, 2, 0)[..., None] * half_rows + offsets
    ).reshape(grid.plane, -1)
    own_spots = pick(all_spots, grid.place)
    key_spots = all_spots.reshape(-1)
    line_rows = own_spots.shape[0]

    hidden_line = all_in.astype(F32)
    normed_line = norm_apply(hidden_line, gains_all[0]).astype(BF16)
    projected = jnp.dot(normed_line, attend_full, preferred_element_type=F32)
    cosine, sine_table = rope_tables(own_spots, head_width)
    queries_b = rotate(projected[:, :head_width], cosine, sine_table).astype(BF16)
    pair_pre = projected[:, head_width:]
    pair_b = jnp.where(core == 0, rotate(pair_pre, cosine, sine_table), pair_pre).astype(BF16)
    pair_all = jnp.zeros((grid.plane,) + pair_b.shape, BF16)
    for mask, part in grid.plane_gather(pair_b).items():
        pair_all = put(pair_all, part, grid.place_of(mask))

    def flip(values):
        shaped = values.reshape(grid.plane, 2, line_rows // 2, -1)
        return shaped[:, ::-1].reshape(values.shape)

    pair_other = flip(grid.across(pair_all))
    keys_b = jnp.where(core == 0, pair_all, pair_other).reshape(-1, head_width)
    values_b = jnp.where(core == 0, pair_other, pair_all).reshape(-1, head_width)

    raw_score = lax.dot_general(queries_b, keys_b, LAST, preferred_element_type=F32)
    bent_score = jnp.tanh(raw_score * score_scale / SOFT_CAP)
    allowed = key_spots[None, :] <= own_spots[:, None]
    exp_score = jnp.where(allowed, jnp.exp(SOFT_CAP * bent_score), 0.0)
    row_total = jnp.sum(exp_score, axis=-1, keepdims=True)
    exp_score_b = exp_score.astype(BF16)
    summed = jnp.dot(exp_score_b, values_b, preferred_element_type=F32)
    mixed_b = (summed / row_total).astype(BF16)
    attend_part = lax.dot_general(mixed_b, output_full, LAST, preferred_element_type=F32)
    attend_sum = grid.token_reduce(attend_part)

    hidden = own_in.astype(F32)
    first_sum = hidden + norm_apply(attend_sum, gains_all[1])
    normed_two_b = norm_apply(first_sum, gains_all[2]).astype(BF16)
    normed_two_line = grid.token_gather(normed_two_b)
    gate_up = jnp.dot(normed_two_line, expand_full, preferred_element_type=F32)
    gate_act = gate_up[:, :quarter]
    up_act = gate_up[:, quarter:]
    inner_b = gate_product(gate_act, up_act).astype(BF16)
    feed_part = lax.dot_general(inner_b, shrink_full, LAST, preferred_element_type=F32)
    feed_sum = grid.token_reduce(feed_part)
    own_hidden_out = (first_sum + norm_apply(feed_sum, gains_all[3])).astype(BF16)

    grad_out = own_out.astype(F32)
    grad_feed, gain_four = norm_back(feed_sum, gains_all[3], grad_out)
    grad_feed_line = grid.token_gather(grad_feed.astype(BF16))
    grad_inner = jnp.dot(grad_feed_line, shrink_full, preferred_element_type=F32)
    _, pull_back = jax.vjp(gate_product, gate_act, up_act)
    grad_gate, grad_up = pull_back(grad_inner)
    grad_gate_up_b = jnp.concatenate([grad_gate, grad_up], axis=1).astype(BF16)
    grad_two_part = lax.dot_general(grad_gate_up_b, expand_full, LAST, preferred_element_type=F32)
    grad_two = grid.token_reduce(grad_two_part)
    shrink_terms = lax.dot_general(
        grad_feed_line, inner_b, ROWS, preferred_element_type=F32
    ).astype(BF16)
    shrink_back = grid.weight_return(shrink_terms)
    expand_terms = lax.dot_general(
        normed_two_line, grad_gate_up_b, ROWS, preferred_element_type=F32
    ).astype(BF16)
    expand_back = grid.weight_return(expand_terms)

    grad_first_norm, gain_three = norm_back(first_sum, gains_all[2], grad_two)
    grad_first = grad_out + grad_first_norm
    grad_attend, gain_two = norm_back(attend_sum, gains_all[1], grad_first)
    grad_attend_line = grid.token_gather(grad_attend.astype(BF16))
    grad_mixed = jnp.dot(grad_attend_line, output_full, preferred_element_type=F32)
    grad_summed_b = (grad_mixed / row_total).astype(BF16)
    row_delta = jnp.sum(grad_mixed * summed, axis=-1, keepdims=True) / (row_total * row_total)
    grad_exp = (
        lax.dot_general(grad_summed_b, values_b, LAST, preferred_element_type=F32) - row_delta
    )
    grad_raw_b = (
        exp_score * grad_exp * (1.0 - bent_score * bent_score) * score_scale
    ).astype(BF16)
    grad_query = jnp.dot(grad_raw_b, keys_b, preferred_element_type=F32)
    grad_key = lax.dot_general(grad_raw_b, queries_b, ROWS, preferred_element_type=F32)
    grad_value = lax.dot_general(exp_score_b, grad_summed_b, ROWS, preferred_element_type=F32)
    pair_shape = (grid.plane, line_rows, head_width)
    kept = jnp.where(core == 0, grad_key, grad_value).reshape(pair_shape)
    given = jnp.where(core == 0, grad_value, grad_key).reshape(pair_shape)
    pair_terms = kept + flip(grid.across(given.astype(BF16))).astype(F32)
    pair_grad = grid.plane_reduce(
        {m: pick(pair_terms, grid.place_of(m)).astype(BF16) for m in range(grid.plane)}
    ).astype(F32)
    grad_query_pre = rotate(grad_query, cosine, -sine_table)
    grad_pair_pre = jnp.where(core == 0, rotate(pair_grad, cosine, -sine_table), pair_grad)
    grad_proj_b = jnp.concatenate([grad_query_pre, grad_pair_pre], axis=1).astype(BF16)
    grad_normed_part = lax.dot_general(grad_proj_b, attend_full, LAST, preferred_element_type=F32)
    grad_normed = grid.token_reduce(grad_normed_part)
    grad_hidden_norm, gain_one = norm_back(hidden, gains_all[0], grad_normed)
    own_hidden_grad = grad_first + grad_hidden_norm

    output_terms = lax.dot_general(
        grad_attend_line, mixed_b, ROWS, preferred_element_type=F32
    ).astype(BF16)
    output_back = core_return(grid.weight_return(output_terms))
    attend_terms = lax.dot_general(
        normed_line, grad_proj_b, ROWS, preferred_element_type=F32
    ).astype(BF16)
    attend_back = core_return(grid.weight_return(attend_terms))

    def both_halves(value):
        other = grid.across(value)
        return jnp.where(
            core == 0, jnp.concatenate([value, other]), jnp.concatenate([other, value])
        )

    hidden_out = both_halves(own_hidden_out)
    hidden_grad = both_halves(own_hidden_grad)

    gain_terms = jnp.stack([gain_one, gain_two, gain_three, gain_four])
    gain_terms = gain_terms + grid.across(gain_terms)
    gain_terms = gain_terms.reshape(-1, LINES, grid.plane, local_width).transpose(1, 2, 0, 3)
    swept = pick(gain_terms, grid.line)
    for step in (1, 2, 3):
        swept = swept + grid.along(pick(gain_terms, grid.line ^ step), step)
    gain_parts = {m: pick(swept, grid.place_of(m)) for m in range(grid.plane)}
    for phase in reversed(range(grid.bits)):
        for mask in range(1 << phase):
            got = grid.within(gain_parts[mask | (1 << phase)], phase)
            gain_parts[mask] = gain_parts[mask] + got
    gains_grad = gain_parts[0]

    attend_grad = (
        attend_back.reshape(2, group_count, local_width, 2, head_width)
        .transpose(2, 1, 3, 0, 4)
        .reshape(attend_weight.shape)
        .astype(F32)
    )
    output_grad = output_back.transpose(1, 0, 3, 2).reshape(output_weight.shape).astype(F32)
    expand_grad = (
        expand_back.reshape(LINES, local_width, 2, quarter)
        .transpose(1, 2, 0, 3)
        .reshape(expand_weight.shape)
        .astype(F32)
    )
    shrink_grad = shrink_back.transpose(0, 2, 1).reshape(shrink_weight.shape).astype(F32)

    attend_after, attend_mean, attend_power = adam_step(
        attend_weight, attend_moment, attend_square, attend_grad, RATE_MATRIX, DECAY
    )
    output_after, output_mean, output_power = adam_step(
        output_weight, output_moment, output_square, output_grad, RATE_MATRIX, DECAY
    )
    expand_after, expand_mean, expand_power = adam_step(
        expand_weight, expand_moment, expand_square, expand_grad, RATE_MATRIX, DECAY
    )
    shrink_after, shrink_mean, shrink_power = adam_step(
        shrink_weight, shrink_moment, shrink_square, shrink_grad, RATE_MATRIX, DECAY
    )
    gains_after, gains_mean, gains_power = adam_step(
        gains_weight, gains_moment, gains_square, gains_grad, RATE_GAIN, 0.0
    )
    return (
        hidden_out,
        hidden_grad,
        attend_grad,
        attend_after,
        attend_mean,
        attend_power,
        output_grad,
        output_after,
        output_mean,
        output_power,
        expand_grad,
        expand_after,
        expand_mean,
        expand_power,
        shrink_grad,
        shrink_after,
        shrink_mean,
        shrink_power,
        gains_grad,
        gains_after,
        gains_mean,
        gains_power,
    )


def solution(mesh):
    tokens = P("ctx", None)
    attend = P("ctx", "head", None, None)
    output = P("head", None, "ctx")
    expand = P("ctx", None, "head")
    shrink = P("head", "ctx")
    gains = P(None, "ctx")
    in_specs = (tokens, tokens, P()) + sum(
        ((spec,) * 3 for spec in (attend, output, expand, shrink, gains)), ()
    )
    out_specs = (tokens, tokens) + sum(
        ((spec,) * 4 for spec in (attend, output, expand, shrink, gains)), ()
    )
    return jax.shard_map(body, mesh=mesh, in_specs=in_specs, out_specs=out_specs, check_vma=False)
```

time: 3500 us -> 846 us (0.24)
  waiting for transfers between devices: 2650 us -> 391 us
  starting transfers between devices: 399 us -> 169 us
  matrix products: 148 us -> 53.9 us
  blocking collectives: 43.2 us -> 0 us
    all_to_all x33 -> x0, waiting for transfers between devices: 1590 us -> none  [send_all(): lax.all_to_all(partial_value.reshape(shard_count, local_width, -1).astype...]
    all_gather x5 -> x0, waiting for transfers between devices: 890 us -> none  [the longest x1 435 us: body(): lax.all_gather(packed[2], 'ctx', axis=0, tiled=True)]
    ppermute x0 -> x107, waiting for transfers between devices: none -> 391 us  [the longest x54 250 us: along(): return lax.ppermute(value, 'ctx', pairs)]
    all_to_all x33 -> x0, starting transfers between devices: 387 us -> none  [send_all(): lax.all_to_all(partial_value.reshape(shard_count, local_width, -1).astype...]
    ppermute x0 -> x107, starting transfers between devices: none -> 169 us  [the longest x54 126 us: along(): return lax.ppermute(value, 'ctx', pairs)]
    unnamed x12 -> x0, waiting for transfers between devices: 128 us -> none
    dot_general x47 -> x18, matrix products: 148 us -> 53.9 us  [the longest x1 8.56 us: body(): lax.dot_general(grad_gate_up_b, expand_full, LAST, preferred_element_type...]
    convert_element_type x34 -> x7, local copies, waits for them, and re-layouts: 80.9 us -> 20.4 us  [the longest x3 20 us: body(): expand_grad = expand_back.reshape(LINES, local_width, 2, quarter).transpo...]
  transfers between devices with their start and end apart: 44 -> 107, of which waited for: 41 -> 56; matrix products, arithmetic and copies ran while one was open for 8% -> 28% of each run, Pallas kernels for 0% -> 0%
where the time goes in v1:
time: 846 us; the launch traced here: 841 us
  waiting for transfers between devices  391 us (46%)
  starting transfers between devices  169 us (20%)
  local copies, waits for them, and re-layouts  150 us (18%)
  other arithmetic  73.8 us (9%)
  matrix products  53.9 us (6%)
    ppermute x54, waiting for transfers between devices, along(): return lax.ppermute(value, 'ctx', pairs)  250 us
    ppermute x36, waiting for transfers between devices, within(): return lax.ppermute(value, ('ctx', 'head'), pairs)  132 us
    ppermute x54, starting transfers between devices, along(): return lax.ppermute(value, 'ctx', pairs)  126 us
    unnamed x188, local copies, waits for them, and re-layouts  51.6 us
    ppermute x36, starting transfers between devices, within(): return lax.ppermute(value, ('ctx', 'head'), pairs)  41.4 us
    sub x5, other arithmetic, adam_step(): weight - rate * (mean_hat / (jnp.sqrt(power_hat) + ADAM_EPS) + decay * we...  21.6 us
    convert_element_type x3, local copies, waits for them, and re-layouts, body(): expand_grad = expand_back.reshape(LINES, local_width, 2, quarter).transpo...  20 us
    dynamic_update_slice x52, local copies, waits for them, and re-layouts, put(): lax.dynamic_update_slice_in_dim(array, jnp.expand_dims(part, dim), index,...  18.9 us
  transfers between devices with their start and end apart: 107, of which 56 were waited for; matrix products, arithmetic and copies ran while one was open for 28% of the time, Pallas kernels for 0%

profile of v1, /device:TPU:0, one launch (start us, length us, event | category | flops | bytes accessed | tf_op | source)
XLA Modules:
  0.0 840.7 jit_solution(11088781943590072748)
XLA Ops:
  20.3 7.3 reshape.361
  68.5 26.6 %collective-permute-done.22 = bf16[144,256]{1,0:T(8,128)(2,1)S(1)} collective-permute-done((bf16[144,256]{1,0:T(8,128)(2,1)S(1)}, bf16[144,256]{1,0:T(8,128)(2,1)S(1)}, u32[]{:S(2)}, u32[]{:S(2)}) %collective-permute-start.22) | collective-permute-done | bytes 73760 | tf_op jit(solution)/shard_map/ppermute | solution.py:100
  95.1 30.8 %collective-permute-start.23 = (bf16[144,256]{1,0:T(8,128)(2,1)S(1)}, bf16[144,256]{1,0:T(8,128)(2,1)S(1)}, u32[]{:S(2)}, u32[]{:S(2)}) collective-permute-start(bf16[144,256]{1,0:T(8,128)(2,1)S(1)} %get-tuple-element.183), channel_id=1, source_target_pairs={{0,16},{2,18},{4,20},{6,22},{8,24},{10,26},{12,28},{14,30},{16,0},... | collective-permute-start | bytes 221192 | tf_op jit(solution)/shard_map/ppermute | solution.py:100
  139.0 8.1 collective-permute-done.42
  147.1 14.0 %collective-permute-start.44 = (bf16[144,1152]{1,0:T(8,128)(2,1)S(1)}, bf16[144,1152]{1,0:T(8,128)(2,1)S(1)}, u32[]{:S(2)}, u32[]{:S(2)}) collective-permute-start(bf16[144,1152]{1,0:T(8,128)(2,1)S(1)} %bitcast.444), channel_id=1, source_target_pairs={{0,8},{2,10},{4,12},{6,14},{8,0},{10,2},{12,4},{14,6},{16,24},{18,... | collective-permute-start | bytes 995336 | tf_op jit(solution)/shard_map/ppermute | solution.py:100
  161.1 6.4 collective-permute-done.43
  184.1 6.9 collective-permute-done.12
  204.6 15.5 %collective-permute-done.2 = bf16[64,2304]{1,0:T(8,128)(2,1)S(1)} collective-permute-done((bf16[64,2304]{1,0:T(8,128)(2,1)}, bf16[64,2304]{1,0:T(8,128)(2,1)S(1)}, u32[]{:S(2)}, u32[]{:S(2)}) %collective-permute-start.2) | collective-permute-done | bytes 294944 | tf_op jit(solution)/shard_map/ppermute | solution.py:100
  231.2 11.4 %collective-permute-done.16 = bf16[4,144,512]{2,1,0:T(8,128)(2,1)S(1)} collective-permute-done((bf16[4,144,512]{2,1,0:T(8,128)(2,1)S(1)}, bf16[4,144,512]{2,1,0:T(8,128)(2,1)S(1)}, u32[]{:S(2)}, u32[]{:S(2)}) %collective-permute-start.16) | collective-permute-done | bytes 589856 | tf_op jit(solution)/shard_map/ppermute | solution.py:111
  252.2 12.7 %collective-permute-done.17 = bf16[512,256]{1,0:T(8,128)(2,1)S(1)} collective-permute-done((bf16[512,256]{1,0:T(8,128)(2,1)S(1)}, bf16[512,256]{1,0:T(8,128)(2,1)S(1)}, u32[]{:S(2)}, u32[]{:S(2)}) %collective-permute-start.17) | collective-permute-done | bytes 262176 | tf_op jit(solution)/shard_map/ppermute | solution.py:111
  305.3 43.2 %collective-permute-done.47 = bf16[4,144,1152]{2,1,0:T(8,128)(2,1)S(1)} collective-permute-done((bf16[4,144,1152]{2,1,0:T(8,128)(2,1)}, bf16[4,144,1152]{2,1,0:T(8,128)(2,1)S(1)}, u32[]{:S(2)}, u32[]{:S(2)}) %collective-permute-start.47) | collective-permute-done | bytes 1327136 | tf_op jit(solution)/shard_map/ppermute | solution.py:111
  352.5 12.4 %collective-permute-done.29 = bf16[64,2304]{1,0:T(8,128)(2,1)S(1)} collective-permute-done((bf16[64,2304]{1,0:T(8,128)(2,1)S(1)}, bf16[64,2304]{1,0:T(8,128)(2,1)S(1)}, u32[]{:S(2)}, u32[]{:S(2)}) %collective-permute-start.29) | collective-permute-done | bytes 294944 | tf_op jit(solution)/shard_map/ppermute | solution.py:100
  370.2 7.2 collective-permute-done.33
  408.9 7.8 collective-permute-done.50
  437.4 7.3 collective-permute-done.54
  450.3 6.6 collective-permute-done.55
  465.5 8.6 %fusion.19 = f32[512,2304]{1,0:T(8,128)} fusion(bf16[2304,2304]{1,0:T(8,128)(2,1)S(1)} %bitcast.404, bf16[512,1152]{1,0:T(8,128)(2,1)} %get-tuple-element.118, bf16[512,1152]{1,0:T(8,128)(2,1)} %get-tuple-element.117), kind=kOutput, calls=%fused_computation.68 | convolution fusion | flops 5440536576 | bytes 17694720 | tf_op jit(solution)/shard_map/dot_general | solution.py:320
  481.5 8.2 convolution_convert_fusion
  532.5 6.5 collective-permute-done.63
  540.2 17.2 %collective-permute-done.96 = bf16[4,144,1152]{2,1,0:T(8,128)(2,1)S(1)} collective-permute-done((bf16[4,144,1152]{2,1,0:T(8,128)(2,1)S(1)}, bf16[4,144,1152]{2,1,0:T(8,128)(2,1)S(1)}, u32[]{:S(2)}, u32[]{:S(2)}) %collective-permute-start.96) | collective-permute-done | bytes 1327136 | tf_op jit(solution)/shard_map/ppermute | solution.py:111
  573.3 15.2 %collective-permute-done.98 = bf16[144,1152]{1,0:T(8,128)(2,1)S(1)} collective-permute-done((bf16[144,1152]{1,0:T(8,128)(2,1)S(1)}, bf16[144,1152]{1,0:T(8,128)(2,1)S(1)}, u32[]{:S(2)}, u32[]{:S(2)}) %collective-permute-start.98) | collective-permute-done | bytes 331808 | tf_op jit(solution)/shard_map/ppermute | solution.py:100
  592.3 6.4 multiply_subtract_fusion.1
  609.2 18.7 %collective-permute-done.82 = bf16[4,144,256]{2,1,0:T(8,128)(2,1)S(1)} collective-permute-done((bf16[4,144,256]{2,1,0:T(8,128)(2,1)S(1)}, bf16[4,144,256]{2,1,0:T(8,128)(2,1)S(1)}, u32[]{:S(2)}, u32[]{:S(2)}) %collective-permute-start.82) | collective-permute-done | bytes 294944 | tf_op jit(solution)/shard_map/ppermute | solution.py:111
  681.3 9.2 %collective-permute-done.91 = bf16[144,2304]{1,0:T(8,128)(2,1)S(1)} collective-permute-done((bf16[144,2304]{1,0:T(8,128)(2,1)S(1)}, bf16[144,2304]{1,0:T(8,128)(2,1)S(1)}, u32[]{:S(2)}, u32[]{:S(2)}) %collective-permute-start.91) | collective-permute-done | bytes 663584 | tf_op jit(solution)/shard_map/ppermute | solution.py:100
  691.7 37.3 %collective-permute-done.92 = bf16[144,2304]{1,0:T(8,128)(2,1)S(1)} collective-permute-done((bf16[144,2304]{1,0:T(8,128)(2,1)S(1)}, bf16[144,2304]{1,0:T(8,128)(2,1)S(1)}, u32[]{:S(2)}, u32[]{:S(2)}) %collective-permute-start.92) | collective-permute-done | bytes 663584 | tf_op jit(solution)/shard_map/ppermute | solution.py:100
  733.6 8.3 copy.182
  741.9 7.1 reshape.386
  773.0 11.4 %multiply_subtract_fusion = (f32[144,2,4608]{2,0,1:T(8,128)}, f32[144,2,4608]{2,0,1:T(8,128)}, f32[144,2,4608]{2,0,1:T(8,128)}) fusion(f32[144,2,4608]{2,1,0:T(2,128)S(1)} %bitcast.393, f32[144,2,4608]{2,0,1:T(8,128)S(1)} %bitcast.391, f32[144,2,4608]{2,1,0:T(2,128)} %param.28, f32[144,2,4608]{2,1,0:T(2,128)} %param.29), kind=kLoop, calls=%fused_computation.15 | loop fusion | flops 19906560 | bytes 37158912 | tf_op jit(solution)/shard_map/sub | solution.py:72
  784.4 6.5 copy.197
  790.9 9.1 %copy.198 = f32[144,2,4608]{2,1,0:T(2,128)} copy(f32[144,2,4608]{2,0,1:T(8,128)} %get-tuple-element.81) | data formatting | bytes 10616832
  800.0 6.7 copy.199
  806.8 6.5 copy.200
  (625 shorter events, 430.4 us)
Async XLA Ops:
  1.3 50.0 %collective-permute-start.4 = (f32[1,4,144]{2,1,0:T(4,128)S(1)}, f32[1,4,144]{2,1,0:T(4,128)S(1)}, u32[]{:S(2)}, u32[]{:S(2)}) collective-permute-start(f32[1,4,144]{2,1,0:T(4,128)S(1)} %bitcast_convert_fusion), channel_id=1, source_target_pairs={{0,8},{2,10},{4,12},{6,14},{8,0},{10,2},{12,4},{14,6},{16,24},{18,... | collective-permute-start | bytes 6920 | tf_op jit(solution)/shard_map/ppermute | solution.py:100
  4.4 37.3 %collective-permute-start.5 = (f32[1,4,144]{2,1,0:T(4,128)S(1)}, f32[1,4,144]{2,1,0:T(4,128)S(1)}, u32[]{:S(2)}, u32[]{:S(2)}) collective-permute-start(f32[1,4,144]{2,1,0:T(4,128)S(1)} %bitcast_convert_fusion), channel_id=1, source_target_pairs={{0,24},{2,26},{4,28},{6,30},{8,16},{10,18},{12,20},{14,22},{16,8},... | collective-permute-start | bytes 6920 | tf_op jit(solution)/shard_map/ppermute | solution.py:100
  8.5 128.9 %collective-permute-start = (bf16[64,2304]{1,0:T(8,128)(2,1)S(1)}, bf16[64,2304]{1,0:T(8,128)(2,1)}, u32[]{:S(2)}, u32[]{:S(2)}) collective-permute-start(bf16[64,2304]{1,0:T(8,128)(2,1)S(1)} %get-tuple-element.96), channel_id=1, source_target_pairs={{0,8},{2,10},{4,12},{6,14},{8,0},{10,2},{12,4},{14,6},{16,24},{18,... | collective-permute-start | bytes 884744 | tf_op jit(solution)/shard_map/ppermute | solution.py:100
  9.2 188.6 %collective-permute-start.1 = (bf16[64,2304]{1,0:T(8,128)(2,1)S(1)}, bf16[64,2304]{1,0:T(8,128)(2,1)}, u32[]{:S(2)}, u32[]{:S(2)}) collective-permute-start(bf16[64,2304]{1,0:T(8,128)(2,1)S(1)} %get-tuple-element.96), channel_id=1, source_target_pairs={{0,24},{2,26},{4,28},{6,30},{8,16},{10,18},{12,20},{14,22},{16,8},... | collective-permute-start | bytes 884744 | tf_op jit(solution)/shard_map/ppermute | solution.py:100
  11.9 52.3 %collective-permute-start.21 = (bf16[2,144,256]{2,1,0:T(8,128)(2,1)}, bf16[2,144,256]{2,1,0:T(8,128)(2,1)}, u32[]{:S(2)}, u32[]{:S(2)}) collective-permute-start(bf16[2,144,256]{2,1,0:T(8,128)(2,1)} %get-tuple-element.187), channel_id=1, source_target_pairs={{0,1},{1,0},{2,3},{3,2},{4,5},{5,4},{6,7},{7,6},{8,9},{9,8},{10,11... | collective-permute-start | bytes 442376 | tf_op jit(solution)/shard_map/ppermute | solution.py:103
  60.7 162.3 %collective-permute-start.36 = (bf16[144,2304]{1,0:T(8,128)(2,1)}, bf16[144,2304]{1,0:T(8,128)(2,1)}, u32[]{:S(2)}, u32[]{:S(2)}) collective-permute-start(bf16[144,2304]{1,0:T(8,128)(2,1)} %get-tuple-element.129), channel_id=1, source_target_pairs={{0,24},{2,26},{4,28},{6,30},{8,16},{10,18},{12,20},{14,22},{16,8},... | collective-permute-start | bytes 1990664 | tf_op jit(solution)/shard_map/ppermute | solution.py:100
  63.8 185.0 %collective-permute-start.37 = (bf16[144,2304]{1,0:T(8,128)(2,1)}, bf16[144,2304]{1,0:T(8,128)(2,1)}, u32[]{:S(2)}, u32[]{:S(2)}) collective-permute-start(bf16[144,2304]{1,0:T(8,128)(2,1)} %get-tuple-element.128), channel_id=1, source_target_pairs={{0,16},{2,18},{4,20},{6,22},{8,24},{10,26},{12,28},{14,30},{16,0},... | collective-permute-start | bytes 1990664 | tf_op jit(solution)/shard_map/ppermute | solution.py:100
  95.1 33.1 %collective-permute-start.23 = (bf16[144,256]{1,0:T(8,128)(2,1)S(1)}, bf16[144,256]{1,0:T(8,128)(2,1)S(1)}, u32[]{:S(2)}, u32[]{:S(2)}) collective-permute-start(bf16[144,256]{1,0:T(8,128)(2,1)S(1)} %get-tuple-element.183), channel_id=1, source_target_pairs={{0,16},{2,18},{4,20},{6,22},{8,24},{10,26},{12,28},{14,30},{16,0},... | collective-permute-start | bytes 221192 | tf_op jit(solution)/shard_map/ppermute | solution.py:100
  137.4 30.1 %collective-permute-start.43 = (bf16[144,1152]{1,0:T(8,128)(2,1)S(1)}, bf16[144,1152]{1,0:T(8,128)(2,1)S(1)}, u32[]{:S(2)}, u32[]{:S(2)}) collective-permute-start(bf16[144,1152]{1,0:T(8,128)(2,1)S(1)} %bitcast.445), channel_id=1, source_target_pairs={{0,16},{2,18},{4,20},{6,22},{8,24},{10,26},{12,28},{14,30},{16,0},... | collective-permute-start | bytes 995336 | tf_op jit(solution)/shard_map/ppermute | solution.py:100
  167.4 30.7 %collective-permute-start.25 = (bf16[4,144,256]{2,1,0:T(8,128)(2,1)S(1)}, bf16[4,144,256]{2,1,0:T(8,128)(2,1)S(1)}, u32[]{:S(2)}, u32[]{:S(2)}) collective-permute-start(bf16[4,144,256]{2,1,0:T(8,128)(2,1)S(1)} %bitcast_dynamic-update-slice_fusion.42), channel_id=1, source_target_pairs={{0,2},{1,5},{2,0},{3,7},{4,6},{5,1},{6,4},{7,3},{8,10},{9,13},{10,... | collective-permute-start | bytes 884744 | tf_op jit(solution)/shard_map/ppermute | solution.py:111
  197.8 75.5 %collective-permute-start.38 = (bf16[144,2304]{1,0:T(8,128)(2,1)S(1)}, bf16[144,2304]{1,0:T(8,128)(2,1)S(1)}, u32[]{:S(2)}, u32[]{:S(2)}) collective-permute-start(bf16[144,2304]{1,0:T(8,128)(2,1)S(1)} %copy-done.46), channel_id=1, source_target_pairs={{0,8},{2,10},{4,12},{6,14},{8,0},{10,2},{12,4},{14,6},{16,24},{18,... | collective-permute-start | bytes 1990664 | tf_op jit(solution)/shard_map/ppermute | solution.py:100
  230.0 68.6 %collective-permute-start.45 = (bf16[4,144,1152]{2,1,0:T(8,128)(2,1)S(1)}, bf16[4,144,1152]{2,1,0:T(8,128)(2,1)}, u32[]{:S(2)}, u32[]{:S(2)}) collective-permute-start(bf16[4,144,1152]{2,1,0:T(8,128)(2,1)S(1)} %bitcast_dynamic-update-slice_fusion.22), channel_id=1, source_target_pairs={{0,2},{1,5},{2,0},{3,7},{4,6},{5,1},{6,4},{7,3},{8,10},{9,13},{10,... | collective-permute-start | bytes 3981320 | tf_op jit(solution)/shard_map/ppermute | solution.py:111
  242.6 58.7 %collective-permute-start.46 = (bf16[4,144,1152]{2,1,0:T(8,128)(2,1)S(1)}, bf16[4,144,1152]{2,1,0:T(8,128)(2,1)}, u32[]{:S(2)}, u32[]{:S(2)}) collective-permute-start(bf16[4,144,1152]{2,1,0:T(8,128)(2,1)S(1)} %bitcast_dynamic-update-slice_fusion.22), channel_id=1, source_target_pairs={{0,4},{1,3},{2,6},{3,1},{4,0},{5,7},{6,2},{7,5},{8,12},{9,11},{10,... | collective-permute-start | bytes 3981320 | tf_op jit(solution)/shard_map/ppermute | solution.py:111
  274.2 74.5 %collective-permute-start.39 = (bf16[4,144,2304]{2,1,0:T(8,128)(2,1)}, bf16[4,144,2304]{2,1,0:T(8,128)(2,1)}, u32[]{:S(2)}, u32[]{:S(2)}) collective-permute-start(bf16[4,144,2304]{2,1,0:T(8,128)(2,1)} %bitcast_dynamic-update-slice_fusion.11), channel_id=1, source_target_pairs={{0,2},{1,5},{2,0},{3,7},{4,6},{5,1},{6,4},{7,3},{8,10},{9,13},{10,... | collective-permute-start | bytes 7962632 | tf_op jit(solution)/shard_map/ppermute | solution.py:111
  277.0 91.1 %collective-permute-start.40 = (bf16[4,144,2304]{2,1,0:T(8,128)(2,1)}, bf16[4,144,2304]{2,1,0:T(8,128)(2,1)}, u32[]{:S(2)}, u32[]{:S(2)}) collective-permute-start(bf16[4,144,2304]{2,1,0:T(8,128)(2,1)} %bitcast_dynamic-update-slice_fusion.11), channel_id=1, source_target_pairs={{0,4},{1,3},{2,6},{3,1},{4,0},{5,7},{6,2},{7,5},{8,12},{9,11},{10,... | collective-permute-start | bytes 7962632 | tf_op jit(solution)/shard_map/ppermute | solution.py:111
  298.6 49.9 %collective-permute-start.47 = (bf16[4,144,1152]{2,1,0:T(8,128)(2,1)}, bf16[4,144,1152]{2,1,0:T(8,128)(2,1)S(1)}, u32[]{:S(2)}, u32[]{:S(2)}) collective-permute-start(bf16[4,144,1152]{2,1,0:T(8,128)(2,1)} %collective-permute-done.45), channel_id=1, source_target_pairs={{0,4},{1,3},{2,6},{3,1},{4,0},{5,7},{6,2},{7,5},{8,12},{9,11},{10,... | collective-permute-start | bytes 3981320 | tf_op jit(solution)/shard_map/ppermute | solution.py:111
  304.6 45.6 %collective-permute-start.30 = (bf16[64,2304]{1,0:T(8,128)(2,1)S(1)}, bf16[64,2304]{1,0:T(8,128)(2,1)S(1)}, u32[]{:S(2)}, u32[]{:S(2)}) collective-permute-start(bf16[64,2304]{1,0:T(8,128)(2,1)S(1)} %get-tuple-element.152), channel_id=1, source_target_pairs={{0,8},{2,10},{4,12},{6,14},{8,0},{10,2},{12,4},{14,6},{16,24},{18,... | collective-permute-start | bytes 884744 | tf_op jit(solution)/shard_map/ppermute | solution.py:100
  348.7 39.9 %collective-permute-start.41 = (bf16[4,144,2304]{2,1,0:T(8,128)(2,1)}, bf16[4,144,2304]{2,1,0:T(8,128)(2,1)S(1)}, u32[]{:S(2)}, u32[]{:S(2)}) collective-permute-start(bf16[4,144,2304]{2,1,0:T(8,128)(2,1)} %collective-permute-done.39), channel_id=1, source_target_pairs={{0,4},{1,3},{2,6},{3,1},{4,0},{5,7},{6,2},{7,5},{8,12},{9,11},{10,... | collective-permute-start | bytes 7962632 | tf_op jit(solution)/shard_map/ppermute | solution.py:111
  495.3 44.9 %collective-permute-start.94 = (bf16[4,144,1152]{2,1,0:T(8,128)(2,1)}, bf16[4,144,1152]{2,1,0:T(8,128)(2,1)S(1)}, u32[]{:S(2)}, u32[]{:S(2)}) collective-permute-start(bf16[4,144,1152]{2,1,0:T(8,128)(2,1)} %get-tuple-element.119), channel_id=1, source_target_pairs={{0,4},{1,3},{2,6},{3,1},{4,0},{5,7},{6,2},{7,5},{8,12},{9,11},{10,... | collective-permute-start | bytes 3981320 | tf_op jit(solution)/shard_map/ppermute | solution.py:111
  502.6 66.5 %collective-permute-start.89 = (bf16[4,144,2304]{2,1,0:T(8,128)(2,1)S(1)}, bf16[4,144,2304]{2,1,0:T(8,128)(2,1)S(1)}, u32[]{:S(2)}, u32[]{:S(2)}) collective-permute-start(bf16[4,144,2304]{2,1,0:T(8,128)(2,1)S(1)} %get-tuple-element.116), channel_id=1, source_target_pairs={{0,4},{1,3},{2,6},{3,1},{4,0},{5,7},{6,2},{7,5},{8,12},{9,11},{10,... | collective-permute-start | bytes 7962632 | tf_op jit(solution)/shard_map/ppermute | solution.py:111
  506.1 159.9 %collective-permute-start.88 = (bf16[4,144,2304]{2,1,0:T(8,128)(2,1)}, bf16[4,144,2304]{2,1,0:T(8,128)(2,1)}, u32[]{:S(2)}, u32[]{:S(2)}) collective-permute-start(bf16[4,144,2304]{2,1,0:T(8,128)(2,1)} %get-tuple-element.115), channel_id=1, source_target_pairs={{0,4},{1,3},{2,6},{3,1},{4,0},{5,7},{6,2},{7,5},{8,12},{9,11},{10,... | collective-permute-start | bytes 7962632 | tf_op jit(solution)/shard_map/ppermute | solution.py:111
  525.3 32.1 %collective-permute-start.96 = (bf16[4,144,1152]{2,1,0:T(8,128)(2,1)S(1)}, bf16[4,144,1152]{2,1,0:T(8,128)(2,1)S(1)}, u32[]{:S(2)}, u32[]{:S(2)}) collective-permute-start(bf16[4,144,1152]{2,1,0:T(8,128)(2,1)S(1)} %fusion.10), channel_id=1, source_target_pairs={{0,2},{1,5},{2,0},{3,7},{4,6},{5,1},{6,4},{7,3},{8,10},{9,13},{10,... | collective-permute-start | bytes 3981320 | tf_op jit(solution)/shard_map/ppermute | solution.py:111
  540.2 58.6 %collective-permute-start.64 = (bf16[256,2304]{1,0:T(8,128)(2,1)}, bf16[256,2304]{1,0:T(8,128)(2,1)}, u32[]{:S(2)}, u32[]{:S(2)}) collective-permute-start(bf16[256,2304]{1,0:T(8,128)(2,1)} %pad_maximum_fusion.6), channel_id=1, source_target_pairs={{0,1},{1,0},{2,3},{3,2},{4,5},{5,4},{6,7},{7,6},{8,9},{9,8},{10,11... | collective-permute-start | bytes 3538952 | tf_op jit(solution)/shard_map/ppermute | solution.py:103
  571.4 94.5 %collective-permute-start.90 = (bf16[4,144,2304]{2,1,0:T(8,128)(2,1)}, bf16[4,144,2304]{2,1,0:T(8,128)(2,1)}, u32[]{:S(2)}, u32[]{:S(2)}) collective-permute-start(bf16[4,144,2304]{2,1,0:T(8,128)(2,1)} %fusion.1), channel_id=1, source_target_pairs={{0,2},{1,5},{2,0},{3,7},{4,6},{5,1},{6,4},{7,3},{8,10},{9,13},{10,... | collective-permute-start | bytes 7962632 | tf_op jit(solution)/shard_map/ppermute | solution.py:111
  676.2 78.9 %collective-permute-start.69 = (bf16[256,2304]{1,0:T(8,128)(2,1)}, bf16[256,2304]{1,0:T(8,128)(2,1)}, u32[]{:S(2)}, u32[]{:S(2)}) collective-permute-start(bf16[256,2304]{1,0:T(8,128)(2,1)} %slice.304), channel_id=1, source_target_pairs={{0,1},{1,0},{2,3},{3,2},{4,5},{5,4},{6,7},{7,6},{8,9},{9,8},{10,11... | collective-permute-start | bytes 3538952 | tf_op jit(solution)/shard_map/ppermute | solution.py:103
  676.2 72.8 %collective-permute-start.74 = (bf16[4,144,512]{2,1,0:T(8,128)(2,1)}, bf16[4,144,512]{2,1,0:T(8,128)(2,1)S(1)}, u32[]{:S(2)}, u32[]{:S(2)}) collective-permute-start(bf16[4,144,512]{2,1,0:T(8,128)(2,1)} %get-tuple-element.131), channel_id=1, source_target_pairs={{0,4},{1,3},{2,6},{3,1},{4,0},{5,7},{6,2},{7,5},{8,12},{9,11},{10,... | collective-permute-start | bytes 1769480 | tf_op jit(solution)/shard_map/ppermute | solution.py:111
  677.2 51.7 %collective-permute-start.92 = (bf16[144,2304]{1,0:T(8,128)(2,1)S(1)}, bf16[144,2304]{1,0:T(8,128)(2,1)S(1)}, u32[]{:S(2)}, u32[]{:S(2)}) collective-permute-start(bf16[144,2304]{1,0:T(8,128)(2,1)S(1)} %get-tuple-element.124), channel_id=1, source_target_pairs={{0,16},{2,18},{4,20},{6,22},{8,24},{10,26},{12,28},{14,30},{16,0},... | collective-permute-start | bytes 1990664 | tf_op jit(solution)/shard_map/ppermute | solution.py:100
  677.2 51.8 %collective-permute-start.93 = (bf16[144,2304]{1,0:T(8,128)(2,1)S(1)}, bf16[144,2304]{1,0:T(8,128)(2,1)S(1)}, u32[]{:S(2)}, u32[]{:S(2)}) collective-permute-start(bf16[144,2304]{1,0:T(8,128)(2,1)S(1)} %get-tuple-element.123), channel_id=1, source_target_pairs={{0,8},{2,10},{4,12},{6,14},{8,0},{10,2},{12,4},{14,6},{16,24},{18,... | collective-permute-start | bytes 1990664 | tf_op jit(solution)/shard_map/ppermute | solution.py:100
  690.5 58.5 %collective-permute-start.76 = (bf16[4,144,512]{2,1,0:T(8,128)(2,1)}, bf16[4,144,512]{2,1,0:T(8,128)(2,1)}, u32[]{:S(2)}, u32[]{:S(2)}) collective-permute-start(bf16[4,144,512]{2,1,0:T(8,128)(2,1)} %fusion.21), channel_id=1, source_target_pairs={{0,2},{1,5},{2,0},{3,7},{4,6},{5,1},{6,4},{7,3},{8,10},{9,13},{10,... | collective-permute-start | bytes 1769480 | tf_op jit(solution)/shard_map/ppermute | solution.py:111
  758.3 56.1 %collective-permute-start.70 = (bf16[64,2304]{1,0:T(8,128)(2,1)}, bf16[64,2304]{1,0:T(8,128)(2,1)}, u32[]{:S(2)}, u32[]{:S(2)}) collective-permute-start(bf16[64,2304]{1,0:T(8,128)(2,1)} %get-tuple-element.145), channel_id=1, source_target_pairs={{0,8},{2,10},{4,12},{6,14},{8,0},{10,2},{12,4},{14,6},{16,24},{18,... | collective-permute-start | bytes 884744 | tf_op jit(solution)/shard_map/ppermute | solution.py:100
  765.2 48.2 %collective-permute-start.80 = (bf16[2,144,512]{2,1,0:T(8,128)(2,1)}, bf16[2,144,512]{2,1,0:T(8,128)(2,1)}, u32[]{:S(2)}, u32[]{:S(2)}) collective-permute-start(bf16[2,144,512]{2,1,0:T(8,128)(2,1)} %get-tuple-element.161), channel_id=1, source_target_pairs={{0,1},{1,0},{2,3},{3,2},{4,5},{5,4},{6,7},{7,6},{8,9},{9,8},{10,11... | collective-permute-start | bytes 884744 | tf_op jit(solution)/shard_map/ppermute | solution.py:103
  771.4 43.0 %collective-permute-start.72 = (bf16[64,2304]{1,0:T(8,128)(2,1)}, bf16[64,2304]{1,0:T(8,128)(2,1)}, u32[]{:S(2)}, u32[]{:S(2)}) collective-permute-start(bf16[64,2304]{1,0:T(8,128)(2,1)} %fusion.44), channel_id=1, source_target_pairs={{0,24},{2,26},{4,28},{6,30},{8,16},{10,18},{12,20},{14,22},{16,8},... | collective-permute-start | bytes 884744 | tf_op jit(solution)/shard_map/ppermute | solution.py:100
  (156 other events, 2221.7 us)
